TPU v7x, 512 devices: a whole 4x4x16 slice. The times are simulated.
512 devices in a mesh: row: 32 (over y, z_lo), col: 16 (over z_hi, x, core).
Axes of the slice: x: 4, y: 4, z: 16 (z_hi: 2, z_lo: 8; z = z_hi * 8 + z_lo), core: 2. Of those that a mesh axis runs over, the one named last changes fastest.
Arguments:
- features: bfloat16 [32, 16, 4, 128, 128], P('row', 'col'), may hold values from -6 to 6
- adjacency: bfloat16 [32, 16, 28, 128, 128], P('row', 'col'), may hold values from 0 to 30, as said below
- edge_dst: int32 [32, 16, 28], P('row', 'col'), may hold values from 0 to 3
- edge_src: int32 [32, 16, 28], P('row', 'col'), may hold values from 0 to 51
- send_row: int32 [32, 16, 32, 1], P('row', 'col'), may hold values from 0 to 3
- send_col: int32 [32, 16, 16, 1], P('row', 'col'), may hold values from 0 to 3
- w_self1: bfloat16 [128, 128], replicated, may hold values from -0.5 to 0.5
- w_neigh1: bfloat16 [128, 128], replicated, may hold values from -1.5 to 1.5
- w_self2: bfloat16 [128, 128], replicated, may hold values from -0.5 to 0.5
- w_neigh2: bfloat16 [128, 128], replicated, may hold values from -1.5 to 1.5
- cotangent: bfloat16 [32, 16, 4, 128, 128], P('row', 'col'), may hold values from -6 to 6
Outputs:
- output: bfloat16 [32, 16, 4, 128, 128], P('row', 'col')
- grad_features: float32 [32, 16, 4, 128, 128], P('row', 'col')
- grad_self1: float32 [128, 128], replicated
- grad_neigh1: float32 [128, 128], replicated
- grad_self2: float32 [128, 128], replicated
- grad_neigh2: float32 [128, 128], replicated
Inputs may be any that keep to these rules, and one draw needn't show every extreme that they name: send_row[r, c, p] lists the own blocks that device (r, c) sends to device (p, c), in slot order. send_col[r, c, q] lists the own blocks that device (r, c) sends to device (r, q), in slot order. `adjacency`: edge weights are nonnegative.
All inputs are finite; a program needn't handle non-finite values.
Results may differ from a plain program's by a relative error of at most 0.0059.
Values may be sent and summed in bfloat16 or wider, within the bound.
A program may use at most 64 MiB of HBM per device.

v0:
```python
import math

import jax
import jax.numpy as jnp
from jax import lax
from jax.sharding import PartitionSpec as P

HIGHEST = lax.Precision.HIGHEST


def silu_slope(pre):
    sigmoid = jax.nn.sigmoid(pre)
    return sigmoid * (1.0 + pre * (1.0 - sigmoid))


def boundary_table(own_blocks, row_list, col_list):
    row_recv = lax.all_to_all(
        own_blocks[row_list.reshape(-1)], "row", split_axis=0, concat_axis=0, tiled=True
    )
    col_recv = lax.all_to_all(
        own_blocks[col_list.reshape(-1)], "col", split_axis=0, concat_axis=0, tiled=True
    )
    return jnp.concatenate([own_blocks, row_recv, col_recv], axis=0)


def local(
    features,
    adjacency,
    edge_dst,
    edge_src,
    send_row,
    send_col,
    w_self1,
    w_neigh1,
    w_self2,
    w_neigh2,
    cotangent,
):
    own_in = features[0, 0]
    adj_tiles = adjacency[0, 0]
    dst_index = edge_dst[0, 0]
    src_index = edge_src[0, 0]
    row_list = send_row[0, 0]
    col_list = send_col[0, 0]
    own_count = own_in.shape[0]
    block_rows = own_in.shape[1]
    feat_width = own_in.shape[2]
    table_size = own_count + row_list.size + col_list.size
    dst_hot = (dst_index[None, :] == jnp.arange(own_count, dtype=jnp.int32)[:, None]).astype(
        jnp.float32
    )
    src_hot = (src_index[None, :] == jnp.arange(table_size, dtype=jnp.int32)[:, None]).astype(
        jnp.float32
    )
    row_hot = (
        row_list.reshape(-1)[None, :] == jnp.arange(own_count, dtype=jnp.int32)[:, None]
    ).astype(jnp.float32)
    col_hot = (
        col_list.reshape(-1)[None, :] == jnp.arange(own_count, dtype=jnp.int32)[:, None]
    ).astype(jnp.float32)
    row_sums = jnp.einsum(
        "eij,j->ei",
        adj_tiles,
        jnp.ones((block_rows,), jnp.bfloat16),
        preferred_element_type=jnp.float32,
    )
    degree = 1.0 + jnp.dot(dst_hot, row_sums, precision=HIGHEST)
    degree_flat = degree.reshape(-1)

    def aggregate(layer_in):
        table = boundary_table(layer_in, row_list, col_list)
        products = jnp.einsum(
            "eij,ejh->eih", adj_tiles, table[src_index], preferred_element_type=jnp.float32
        )
        summed = jnp.einsum("be,eih->bih", dst_hot, products, precision=HIGHEST)
        return ((layer_in.astype(jnp.float32) + summed) / degree[:, :, None]).astype(jnp.bfloat16)

    def spread(q_blocks):
        contrib = jnp.einsum(
            "eji,ejh->eih", adj_tiles, q_blocks[dst_index], preferred_element_type=jnp.float32
        )
        table_grad = jnp.einsum("te,eih->tih", src_hot, contrib, precision=HIGHEST)
        row_end = own_count + row_list.size
        from_row = lax.all_to_all(
            table_grad[own_count:row_end], "row", split_axis=0, concat_axis=0, tiled=True
        )
        from_col = lax.all_to_all(
            table_grad[row_end:], "col", split_axis=0, concat_axis=0, tiled=True
        )
        returned = table_grad[:own_count] + q_blocks.astype(jnp.float32)
        returned = returned + jnp.einsum("br,rih->bih", row_hot, from_row, precision=HIGHEST)
        returned = returned + jnp.einsum("br,rih->bih", col_hot, from_col, precision=HIGHEST)
        return returned

    mean_one = aggregate(own_in)
    flat_in = own_in.reshape(-1, feat_width)
    mean_one_flat = mean_one.reshape(-1, feat_width)
    pre_one = jnp.dot(flat_in, w_self1, preferred_element_type=jnp.float32) + jnp.dot(
        mean_one_flat, w_neigh1, preferred_element_type=jnp.float32
    )
    hidden = jax.nn.silu(pre_one).astype(jnp.bfloat16)
    hidden_blocks = hidden.reshape(own_in.shape)
    mean_two = aggregate(hidden_blocks)
    mean_two_flat = mean_two.reshape(-1, feat_width)
    output = (
        jnp.dot(hidden, w_self2, preferred_element_type=jnp.float32)
        + jnp.dot(mean_two_flat, w_neigh2, preferred_element_type=jnp.float32)
    ).astype(jnp.bfloat16)
    cot_flat = cotangent[0, 0].reshape(-1, feat_width)
    grad_scale = 1.0 / math.sqrt(
        own_count * block_rows * lax.axis_size("row") * lax.axis_size("col")
    )
    g_self2 = jnp.einsum("nh,nk->hk", hidden, cot_flat, preferred_element_type=jnp.float32)
    g_neigh2 = jnp.einsum("nh,nk->hk", mean_two_flat, cot_flat, preferred_element_type=jnp.float32)
    q_two = (
        jnp.dot(cot_flat, w_neigh2.T, preferred_element_type=jnp.float32) / degree_flat[:, None]
    ).astype(jnp.bfloat16)
    back_two = spread(q_two.reshape(own_in.shape))
    dhidden = jnp.dot(cot_flat, w_self2.T, preferred_element_type=jnp.float32) + back_two.reshape(
        -1, feat_width
    )
    dpre_one = (dhidden * silu_slope(pre_one)).astype(jnp.bfloat16)
    g_self1 = jnp.einsum("nh,nk->hk", flat_in, dpre_one, preferred_element_type=jnp.float32)
    g_neigh1 = jnp.einsum("nh,nk->hk", mean_one_flat, dpre_one, preferred_element_type=jnp.float32)
    q_one = (
        jnp.dot(dpre_one, w_neigh1.T, preferred_element_type=jnp.float32) / degree_flat[:, None]
    ).astype(jnp.bfloat16)
    back_one = spread(q_one.reshape(own_in.shape))
    grad_in = jnp.dot(dpre_one, w_self1.T, preferred_element_type=jnp.float32) + back_one.reshape(
        -1, feat_width
    )
    g_self1, g_neigh1, g_self2, g_neigh2 = lax.psum(
        (g_self1, g_neigh1, g_self2, g_neigh2), ("row", "col")
    )
    return (
        output.reshape(features.shape),
        grad_in.reshape(features.shape),
        g_self1 * grad_scale,
        g_neigh1 * grad_scale,
        g_self2 * grad_scale,
        g_neigh2 * grad_scale,
    )


def solution(mesh):
    placed = (
        P("row", "col", None, None, None),
        P("row", "col", None, None, None),
        P("row", "col", None),
        P("row", "col", None),
        P("row", "col", None, None),
        P("row", "col", None, None),
        P(),
        P(),
        P(),
        P(),
        P("row", "col", None, None, None),
    )
    return jax.shard_map(
        local,
        mesh=mesh,
        in_specs=placed,
        out_specs=(
            P("row", "col", None, None, None),
            P("row", "col", None, None, None),
            P(),
            P(),
            P(),
            P(),
        ),
        check_vma=False,
    )
```

profile of v0, /device:TPU:1, one launch (start us, length us, event | category | flops | bytes accessed | tf_op | source)
XLA Modules:
  0.0 989.4 jit_solution(9908587097664640978)
XLA Ops:
  8.0 2.3 gather_fusion.1
  10.3 19.1 %all-to-all-start.1 = ((bf16[16,128,128]{2,1,0:T(8,128)(2,1)}), bf16[16,128,128]{2,1,0:T(8,128)(2,1)S(1)}, u32[]{:S(2)}, u32[]{:S(2)}) async-start(bf16[16,128,128]{2,1,0:T(8,128)(2,1)} %gather_fusion.1), calls=%async_computation.1 | async-start | bytes 1048576 | tf_op jit(solution)/shard_map/all_to_all | solution.py:20
  31.1 17.6 %all-to-all-done.1 = bf16[16,128,128]{2,1,0:T(8,128)(2,1)S(1)} async-done(((bf16[16,128,128]{2,1,0:T(8,128)(2,1)}), bf16[16,128,128]{2,1,0:T(8,128)(2,1)S(1)}, u32[]{:S(2)}, u32[]{:S(2)}) %all-to-all-start.1) | async-done | bytes 524320 | tf_op jit(solution)/shard_map/all_to_all | solution.py:20
  48.7 23.5 %all-to-all-start = ((bf16[32,128,128]{2,1,0:T(8,128)(2,1)}), bf16[32,128,128]{2,1,0:T(8,128)(2,1)}, u32[]{:S(2)}, u32[]{:S(2)}) async-start(bf16[32,128,128]{2,1,0:T(8,128)(2,1)} %gather_fusion), calls=%async_computation | async-start | bytes 2097152 | tf_op jit(solution)/shard_map/all_to_all | solution.py:17
  75.4 2.4 copy.124
  82.8 39.7 %all-to-all-done = bf16[32,128,128]{2,1,0:T(8,128)(2,1)} async-done(((bf16[32,128,128]{2,1,0:T(8,128)(2,1)}), bf16[32,128,128]{2,1,0:T(8,128)(2,1)}, u32[]{:S(2)}, u32[]{:S(2)}) %all-to-all-start) | async-done | bytes 1048608 | tf_op jit(solution)/shard_map/all_to_all | solution.py:17
  122.5 5.8 all-to-all-start.5
  132.4 3.2 convolution_bitcast_fusion.3
  135.6 2.4 copy.118
  141.3 32.3 %all-to-all-done.5 = f32[16,128,128]{2,1,0:T(8,128)} async-done(((f32[16,128,128]{2,1,0:T(8,128)}), f32[16,128,128]{2,1,0:T(8,128)}, u32[]{:S(2)}, u32[]{:S(2)}) %all-to-all-start.5) | async-done | bytes 1048608 | tf_op jit(solution)/shard_map/all_to_all | solution.py:87
  173.6 9.1 all-to-all-start.3
  184.8 2.6 copy.126
  187.4 14.6 %all-to-all-done.3 = bf16[16,128,128]{2,1,0:T(8,128)(2,1)} async-done(((bf16[16,128,128]{2,1,0:T(8,128)(2,1)}), bf16[16,128,128]{2,1,0:T(8,128)(2,1)}, u32[]{:S(2)}, u32[]{:S(2)}) %all-to-all-start.3) | async-done | bytes 524320 | tf_op jit(solution)/shard_map/all_to_all | solution.py:20
  202.1 23.0 %all-to-all-start.4 = ((f32[32,128,128]{2,1,0:T(8,128)}), f32[32,128,128]{2,1,0:T(8,128)S(1)}, u32[]{:S(2)}, u32[]{:S(2)}) async-start(f32[32,128,128]{2,1,0:T(8,128)} %copy.126), calls=%async_computation.4 | async-start | bytes 4194304 | tf_op jit(solution)/shard_map/all_to_all | solution.py:84
  226.8 90.8 %all-to-all-done.4 = f32[32,128,128]{2,1,0:T(8,128)S(1)} async-done(((f32[32,128,128]{2,1,0:T(8,128)}), f32[32,128,128]{2,1,0:T(8,128)S(1)}, u32[]{:S(2)}, u32[]{:S(2)}) %all-to-all-start.4) | async-done | bytes 2097184 | tf_op jit(solution)/shard_map/all_to_all | solution.py:84
  317.6 9.3 all-to-all-start.2
  327.0 3.1 fusion.4
  330.0 2.2 convolution_add_fusion.2
  335.2 2.4 copy.132
  341.2 2.6 copy.134
  343.8 33.3 %all-to-all-done.2 = bf16[32,128,128]{2,1,0:T(8,128)(2,1)} async-done(((bf16[32,128,128]{2,1,0:T(8,128)(2,1)}), bf16[32,128,128]{2,1,0:T(8,128)(2,1)}, u32[]{:S(2)}, u32[]{:S(2)}) %all-to-all-start.2) | async-done | bytes 1048608 | tf_op jit(solution)/shard_map/all_to_all | solution.py:17
  377.1 6.1 all-to-all-start.6
  386.0 89.7 %all-to-all-done.6 = f32[32,128,128]{2,1,0:T(8,128)S(1)} async-done(((f32[32,128,128]{2,1,0:T(8,128)}), f32[32,128,128]{2,1,0:T(8,128)S(1)}, u32[]{:S(2)}, u32[]{:S(2)}) %all-to-all-start.6) | async-done | bytes 2097184 | tf_op jit(solution)/shard_map/all_to_all | solution.py:84
  475.7 10.0 %all-to-all-start.7 = ((f32[16,128,128]{2,1,0:T(8,128)}), f32[16,128,128]{2,1,0:T(8,128)}, u32[]{:S(2)}, u32[]{:S(2)}) async-start(f32[16,128,128]{2,1,0:T(8,128)} %copy.136), calls=%async_computation.7 | async-start | bytes 2097152 | tf_op jit(solution)/shard_map/all_to_all | solution.py:87
  489.4 2.9 pad_maximum_fusion.1
  492.3 3.0 gather_fusion.5
  495.4 3.2 convolution_bitcast_fusion.2
  498.6 3.1 copy.121
  504.3 2.4 fusion.43
  509.6 461.4 %all-reduce.3.cloned.1.call-done = (f32[128,128]{0,1:T(8,128)}, f32[128,128]{0,1:T(8,128)}, f32[128,128]{0,1:T(8,128)}, f32[128,128]{0,1:T(8,128)}) async-done(((f32[128,128]{0,1:T(8,128)}, f32[128,128]{0,1:T(8,128)}, f32[128,128]{0,1:T(8,128)}, f32[128,128]{0,1:T(8,128)}), (f32[128,128]{0,1:T(8,128)}, f32[128,128]{0,1:T(8,128)}, f32[128,128]{0,1:T(8,128)}, ...) | async-done | bytes 262160 | tf_op jit(solution)/shard_map/psum | solution.py:132
  975.6 3.7 fusion.7
  979.3 2.3 convolution_add_fusion
  (103 shorter events, 45.7 us)
Async XLA Ops:
  7.2 65.0 %copy-start = (bf16[1,1,28,128,128]{4,3,2,1,0:T(8,128)(2,1)S(1)}, bf16[1,1,28,128,128]{4,3,2,1,0:T(8,128)(2,1)}, u32[]{:S(2)}) copy-start(bf16[1,1,28,128,128]{4,3,2,1,0:T(8,128)(2,1)} %param.12) | copy-start | bytes 2752516
  7.2 22.2 %copy-start.1 = (bf16[1,1,4,128,128]{4,3,2,1,0:T(8,128)(2,1)S(1)}, bf16[1,1,4,128,128]{4,3,2,1,0:T(8,128)(2,1)}, u32[]{:S(2)}) copy-start(bf16[1,1,4,128,128]{4,3,2,1,0:T(8,128)(2,1)} %param.11) | copy-start | bytes 393220
  7.2 22.2 %copy-start.18 = (s32[1,1,32,1]{2,3,1,0:T(1,128)S(1)}, s32[1,1,32,1]{2,3,1,0:T(1,128)}, u32[]{:S(2)}) copy-start(s32[1,1,32,1]{2,3,1,0:T(1,128)} %param.15) | copy-start | bytes 388
  10.3 38.4 %all-to-all-start.1 = ((bf16[16,128,128]{2,1,0:T(8,128)(2,1)}), bf16[16,128,128]{2,1,0:T(8,128)(2,1)S(1)}, u32[]{:S(2)}, u32[]{:S(2)}) async-start(bf16[16,128,128]{2,1,0:T(8,128)(2,1)} %gather_fusion.1), calls=%async_computation.1 | async-start | bytes 1048576 | tf_op jit(solution)/shard_map/all_to_all | solution.py:20
  29.4 42.8 %copy-start.15 = (s32[1,1,28]{2,1,0:T(1,128)S(1)}, s32[1,1,28]{2,1,0:T(1,128)}, u32[]{:S(2)}) copy-start(s32[1,1,28]{2,1,0:T(1,128)} %param.13) | copy-start | bytes 340
  29.4 43.3 %copy-start.6 = (bf16[1,1,4,128,128]{4,3,2,1,0:T(8,128)(2,1)S(1)}, bf16[1,1,4,128,128]{4,3,2,1,0:T(8,128)(2,1)}, u32[]{:S(2)}) copy-start(bf16[1,1,4,128,128]{4,3,2,1,0:T(8,128)(2,1)} %param.21) | copy-start | bytes 393220
  29.4 43.3 %copy-start.13 = (bf16[128,128]{1,0:T(8,128)(2,1)S(1)}, bf16[128,128]{1,0:T(8,128)(2,1)}, u32[]{:S(2)}) copy-start(bf16[128,128]{1,0:T(8,128)(2,1)} %param.20) | copy-start | bytes 98308
  48.7 24.2 %copy-start.4 = (bf16[16,128,128]{2,1,0:T(8,128)(2,1)}, bf16[16,128,128]{2,1,0:T(8,128)(2,1)S(1)}, u32[]{:S(2)}) copy-start(bf16[16,128,128]{2,1,0:T(8,128)(2,1)S(1)} %all-to-all-done.1) | copy-start | bytes 1572868
  48.7 73.8 %all-to-all-start = ((bf16[32,128,128]{2,1,0:T(8,128)(2,1)}), bf16[32,128,128]{2,1,0:T(8,128)(2,1)}, u32[]{:S(2)}, u32[]{:S(2)}) async-start(bf16[32,128,128]{2,1,0:T(8,128)(2,1)} %gather_fusion), calls=%async_computation | async-start | bytes 2097152 | tf_op jit(solution)/shard_map/all_to_all | solution.py:17
  75.4 2.4 copy-start.16
  79.6 1.8 copy-start.3
  81.5 46.9 %copy-start.11 = (bf16[128,128]{1,0:T(8,128)(2,1)S(1)}, bf16[128,128]{1,0:T(8,128)(2,1)}, u32[]{:S(2)}) copy-start(bf16[128,128]{1,0:T(8,128)(2,1)} %param.17) | copy-start | bytes 98308
  81.5 47.8 %copy-start.5 = (bf16[16,128,128]{2,1,0:T(8,128)(2,1)S(1)}, bf16[16,128,128]{2,1,0:T(8,128)(2,1)}, u32[]{:S(2)}) copy-start(bf16[16,128,128]{2,1,0:T(8,128)(2,1)} %copy-done.4) | copy-start | bytes 1572868
  122.5 51.1 %all-to-all-start.5 = ((f32[16,128,128]{2,1,0:T(8,128)}), f32[16,128,128]{2,1,0:T(8,128)}, u32[]{:S(2)}, u32[]{:S(2)}) async-start(f32[16,128,128]{2,1,0:T(8,128)} %copy.128), calls=%async_computation.5 | async-start | bytes 2097152 | tf_op jit(solution)/shard_map/all_to_all | solution.py:87
  139.0 34.6 %copy-start.9 = (bf16[4,128,128]{2,1,0:T(8,128)(2,1)}, bf16[4,128,128]{2,1,0:T(8,128)(2,1)S(1)}, u32[]{:S(2)}) copy-start(bf16[4,128,128]{2,1,0:T(8,128)(2,1)S(1)} %fusion.26) | copy-start | bytes 393220
  173.6 28.4 %all-to-all-start.3 = ((bf16[16,128,128]{2,1,0:T(8,128)(2,1)}), bf16[16,128,128]{2,1,0:T(8,128)(2,1)}, u32[]{:S(2)}, u32[]{:S(2)}) async-start(bf16[16,128,128]{2,1,0:T(8,128)(2,1)} %gather_fusion.4), calls=%async_computation.3 | async-start | bytes 1048576 | tf_op jit(solution)/shard_map/all_to_all | solution.py:20
  202.1 115.5 %all-to-all-start.4 = ((f32[32,128,128]{2,1,0:T(8,128)}), f32[32,128,128]{2,1,0:T(8,128)S(1)}, u32[]{:S(2)}, u32[]{:S(2)}) async-start(f32[32,128,128]{2,1,0:T(8,128)} %copy.126), calls=%async_computation.4 | async-start | bytes 4194304 | tf_op jit(solution)/shard_map/all_to_all | solution.py:84
  226.8 103.3 %copy-start.20 = (s32[1,1,16,1]{2,3,1,0:T(1,128)S(1)}, s32[1,1,16,1]{2,3,1,0:T(1,128)}, u32[]{:S(2)}) copy-start(s32[1,1,16,1]{2,3,1,0:T(1,128)} %param.16) | copy-start | bytes 196
  317.6 59.5 %all-to-all-start.2 = ((bf16[32,128,128]{2,1,0:T(8,128)(2,1)}), bf16[32,128,128]{2,1,0:T(8,128)(2,1)}, u32[]{:S(2)}, u32[]{:S(2)}) async-start(bf16[32,128,128]{2,1,0:T(8,128)(2,1)} %gather_fusion.3), calls=%async_computation.2 | async-start | bytes 2097152 | tf_op jit(solution)/shard_map/all_to_all | solution.py:17
  326.9 5.4 copy-start.7
  326.9 5.4 copy-start.14
  326.9 5.4 copy-start.24
  330.0 2.5 copy-start.23
  335.2 2.4 copy-start.17
  339.4 1.8 copy-start.2
  377.1 98.6 %all-to-all-start.6 = ((f32[32,128,128]{2,1,0:T(8,128)}), f32[32,128,128]{2,1,0:T(8,128)S(1)}, u32[]{:S(2)}, u32[]{:S(2)}) async-start(f32[32,128,128]{2,1,0:T(8,128)} %copy.134), calls=%async_computation.6 | async-start | bytes 4194304 | tf_op jit(solution)/shard_map/all_to_all | solution.py:84
  475.7 503.6 %all-to-all-start.7 = ((f32[16,128,128]{2,1,0:T(8,128)}), f32[16,128,128]{2,1,0:T(8,128)}, u32[]{:S(2)}, u32[]{:S(2)}) async-start(f32[16,128,128]{2,1,0:T(8,128)} %copy.136), calls=%async_computation.7 | async-start | bytes 2097152 | tf_op jit(solution)/shard_map/all_to_all | solution.py:87
  485.8 485.1 %all-reduce.3.cloned.1.call-start = ((), (), s32[]{:S(2)}) async-start(), calls=%async_computation.8 | async-start | bytes 524288 | tf_op jit(solution)/shard_map/psum | solution.py:132
  501.7 5.2 copy-start.8
  504.3 471.3 %copy-start.19 = (s32[1,1,32,1]{2,3,1,0:T(1,128)S(1)}, s32[1,1,32,1]{2,3,1,0:T(1,128)}, u32[]{:S(2)}) copy-start(s32[1,1,32,1]{2,3,1,0:T(1,128)} %param.15) | copy-start | bytes 388
  509.6 469.8 %copy-start.21 = (s32[1,1,16,1]{2,3,1,0:T(1,128)S(1)}, s32[1,1,16,1]{2,3,1,0:T(1,128)}, u32[]{:S(2)}) copy-start(s32[1,1,16,1]{2,3,1,0:T(1,128)} %param.16) | copy-start | bytes 196
  975.6 6.0 copy-start.12
  (2 other events, 2.0 us)
Sparse Core Ops, SparseCore 0:
  507.9 462.9 all-reduce.2
where the time goes:
time: 991 us; the launch traced here: 989 us
  waiting for transfers between devices  779 us (79%)
  starting transfers between devices  106 us (11%)
  local copies, waits for them, and re-layouts  41.7 us (4%)
  matrix products  40.4 us (4%)
  between operations  14.6 us (1%)
    psum x1, waiting for transfers between devices, local(): lax.psum((g_self1, g_neigh1, g_self2, g_neigh2), ('row', 'col'))  461 us
    all_to_all x2, waiting for transfers between devices, spread(): lax.all_to_all(table_grad[own_count:row_end], 'row', split_axis=0, concat...  181 us
    all_to_all x2, waiting for transfers between devices, boundary_table(): lax.all_to_all(own_blocks[row_list.reshape(-1)], 'row', split_axis=0, con...  73 us
    all_to_all x2, starting transfers between devices, boundary_table(): lax.all_to_all(own_blocks[row_list.reshape(-1)], 'row', split_axis=0, con...  32.8 us
    all_to_all x2, waiting for transfers between devices, spread(): lax.all_to_all(table_grad[row_end:], 'col', split_axis=0, concat_axis=0,...  32.3 us
    all_to_all x2, waiting for transfers between devices, boundary_table(): lax.all_to_all(own_blocks[col_list.reshape(-1)], 'col', split_axis=0, con...  32.2 us
    all_to_all x2, starting transfers between devices, spread(): lax.all_to_all(table_grad[own_count:row_end], 'row', split_axis=0, concat...  29.1 us
    all_to_all x2, starting transfers between devices, boundary_table(): lax.all_to_all(own_blocks[col_list.reshape(-1)], 'col', split_axis=0, con...  28.2 us
  transfers between devices with their start and end apart: 9, of which 8 were waited for; matrix products, arithmetic and copies ran while one was open for 8% of the time, Pallas kernels for 0%

commit v1 on v0

v1 whole, which is shorter than its diff:
```python
import functools
import math

import jax
import jax.numpy as jnp
from jax import lax
from jax.experimental import pallas as pl
from jax.experimental.pallas import tpu as pltpu
from jax.sharding import PartitionSpec as P

MESH = pl.DeviceIdType.MESH
BF16 = jnp.bfloat16
F32 = jnp.float32
LIMIT = 44 * 1024 * 1024
SPLIT = {"y": 4, "z": 8, "zh": 2, "xc": 8}
LAG = 3


def dot(a, b):
    return jnp.dot(a, b, preferred_element_type=F32)


def dot_bt(a, b):
    return lax.dot_general(a, b, (((1,), (1,)), ((), ())), preferred_element_type=F32)


def dot_at(a, b):
    return lax.dot_general(a, b, (((0,), (0,)), ((), ())), preferred_element_type=F32)


def exchange_kernel(split, with_sum, *refs):
    ny, nz, nh, nx = split["y"], split["z"], split["zh"], split["xc"]
    nrow, ncol = ny * nz, nh * nx
    refs = list(refs)
    own, gsend, idx = refs[:3]
    del refs[:3]
    if with_sum:
        gr = refs.pop(0)
    table, back = refs[:2]
    del refs[:2]
    if with_sum:
        gout = refs.pop(0)
    (chain, far, tiles, pick_row, pick_col, stage_y, stage_c, land_y, land_c, from_left, from_right,
     to_right, to_left, far_out, far_in) = refs[:15]
    (i_s, i_r, f_r, f_sr, f_sl, h_s, h_r, yf_s, yf_r, cf_s, cf_r, yb_s, yb_r, cb_s, cb_r,
     b_rl, b_rr, b_sr, b_sl) = refs[15:34]
    own_count, rows, feat = own.shape

    r = lax.axis_index("row")
    c = lax.axis_index("col")
    y, z = lax.div(r, nz), lax.rem(r, nz)
    zh, xc = lax.div(c, nx), lax.rem(c, nx)

    def y_peer(d):
        return lax.rem(y + d, ny)

    def x_peer(d):
        return lax.rem(xc + d, nx)

    def remote(src, dst, ssem, rsem, row, col):
        return pltpu.make_async_remote_copy(
            src_ref=src, dst_ref=dst, send_sem=ssem, recv_sem=rsem,
            device_id=(row, col), device_id_type=MESH,
        )

    partner = (1 - zh) * nx + xc

    barrier = pltpu.get_barrier_semaphore()

    def greet(row, col):
        pl.semaphore_signal(barrier, inc=1, device_id=(row, col), device_id_type=MESH)

    for d in range(1, ny):
        greet(y_peer(d) * nz + z, c)
    for d in range(1, nz):
        greet(y * nz + lax.rem(z + d, nz), c)
    greet(r, partner)
    for d in range(1, nx):
        greet(r, zh * nx + x_peer(d))
    pl.semaphore_wait(barrier, (ny - 1) + (nz - 1) + 1 + (nx - 1))

    def idx_copy(d):
        zz = lax.rem(z + d, nz)
        return remote(idx, tiles.at[z], i_s.at[d], i_r.at[z], y * nz + zz, c)

    def idx_wait(d):
        zz = lax.rem(z + d, nz)
        return remote(idx, tiles.at[zz], i_s.at[d], i_r.at[zz], y * nz + zz, c)

    idx_far = remote(idx, tiles.at[nz], i_s.at[0], i_r.at[nz], r, partner)
    blocks_far = remote(own, far, h_s.at[0], h_r.at[0], r, partner)
    back_far = remote(far_out, far_in, h_s.at[1], h_r.at[1], r, partner)

    def right(src):
        return remote(chain.at[src], chain.at[src], f_sr.at[src], f_r.at[src], r + 1, c)

    def left(src):
        return remote(chain.at[src], chain.at[src], f_sl.at[src], f_r.at[src], r - 1, c)

    def back_right(o):
        return remote(to_right.at[o], from_left.at[o], b_sr.at[o], b_rl.at[o], r + 1, c)

    def back_left(o):
        return remote(to_left.at[o], from_right.at[o], b_sl.at[o], b_rr.at[o], r - 1, c)

    def y_back(d):
        yy = y_peer(d)
        return remote(gsend.at[pl.ds(yy * nz, nz)], land_y.at[(ny - d) % ny],
                      yb_s.at[d], yb_r.at[(ny - d) % ny], yy * nz + z, c)

    def x_back(d):
        xx = x_peer(d)
        return remote(gsend.at[pl.ds(nrow + xx * nh, nh)], land_c.at[(nx - d) % nx],
                      cb_s.at[d], cb_r.at[(nx - d) % nx], r, zh * nx + xx)

    def y_out(d, src):
        return remote(stage_y.at[d, src], table.at[own_count + y * nz + src],
                      yf_s.at[d, src], yf_r.at[d, src], y_peer(d) * nz + z, c)

    def y_in(d, src):
        yy = lax.rem(y + ny - d, ny)
        return remote(stage_y.at[d, src], table.at[own_count + yy * nz + src],
                      yf_s.at[d, src], yf_r.at[d, src], yy * nz + z, c)

    def col_slot(s, x_from):
        half = zh if s == 0 else 1 - zh
        return own_count + nrow + half * nx + x_from

    def c_out(d, s):
        return remote(stage_c.at[d, s], table.at[col_slot(s, xc)],
                      cf_s.at[d, s], cf_r.at[d, s], r, zh * nx + x_peer(d))

    def c_in(d, s):
        xx = lax.rem(xc + nx - d, nx)
        return remote(stage_c.at[d, s], table.at[col_slot(s, xx)],
                      cf_s.at[d, s], cf_r.at[d, s], r, zh * nx + xx)

    for d in range(1, nz):
        idx_copy(d).start()
    idx_far.start()
    chain[z] = own[...]
    tiles[z] = idx[...]

    @pl.when(z < nz - 1)
    def _():
        right(z).start()

    @pl.when(z > 0)
    def _():
        left(z).start()

    for d in range(1, ny):
        y_back(d).start()
    for d in range(1, nx):
        x_back(d).start()
    blocks_far.start()

    if with_sum:
        ar = sum_stages(split, gr, gout, refs[34:], (r, c, y, z, zh, xc), remote)
        ar[0]()

    table[pl.ds(0, own_count)] = own[...]
    land_y[0] = gsend[pl.ds(y * nz, nz)]
    land_c[0] = gsend[pl.ds(nrow + xc * nh, nh)]

    for d in range(1, nz):
        idx_wait(d).wait_recv()
    idx_far.wait_recv()
    lists = tiles[...].astype(F32)
    along = lists[:nz].reshape(nz * 8, 128).astype(BF16)
    pair = jnp.concatenate([tiles[z].astype(F32), lists[nz]], axis=0).astype(BF16)
    lane = lax.broadcasted_iota(jnp.int32, (128, 128), 0)
    for d in range(ny):
        hot = jnp.where(lane == y_peer(d) * nz + z, 1.0, 0.0).astype(BF16)
        pick_row[d] = dot(along, hot).reshape(nz, 8, 128)
    for d in range(nx):
        hot = jnp.where(lane == nrow + zh * nx + x_peer(d), 1.0, 0.0).astype(BF16)
        pick_col[d] = dot(pair, hot).reshape(2, 8, 128)

    def choose(which, blocks):
        row = which[0:1, :]
        total = None
        for k in range(own_count):
            term = blocks[k].astype(F32) * jnp.where(row == k, 1.0, 0.0)
            total = term if total is None else total + term
        return total.astype(BF16)

    def forward(src):
        blocks = chain.at[src]
        for d in range(ny):
            chosen = choose(pick_row[d, src], blocks)
            if d == 0:
                table[own_count + y * nz + src] = chosen
            else:
                stage_y[d, src] = chosen
                y_out(d, src).start()

    def forward_col(s, blocks):
        for d in range(nx):
            chosen = choose(pick_col[d, s], blocks)
            if d == 0:
                table[col_slot(s, xc)] = chosen
            else:
                stage_c[d, s] = chosen
                c_out(d, s).start()

    def placed(o, k):
        total = None
        for d in range(ny):
            hot = jnp.where(pick_row[d, o][0:1, :] == k, 1.0, 0.0)
            term = land_y[d, o].astype(F32) * hot
            total = term if total is None else total + term
        return total

    def placed_col(half, s, k):
        total = None
        for d in range(nx):
            hot = jnp.where(pick_col[d, s][0:1, :] == k, 1.0, 0.0)
            term = land_c[d, half].astype(F32) * hot
            total = term if total is None else total + term
        return total

    forward(z)
    forward_col(0, own)

    def fwd_step(s):
        src = z - s

        @pl.when(src >= 0)
        def _():
            right(src).wait_recv()

            @pl.when(z < nz - 1)
            def _():
                right(src).start()

            forward(src)

        src2 = z + s

        @pl.when(src2 < nz)
        def _():
            left(src2).wait_recv()

            @pl.when(z > 0)
            def _():
                left(src2).start()

            forward(src2)

    def bwd_step(t):
        o = nz - 1 + z - t

        @pl.when((o > z) & (o < nz))
        def _():
            @pl.when(z > 0)
            def _():
                back_right(o).wait_recv()
                for k in range(own_count):
                    to_right[o, k] = (placed(o, k) + from_left[o, k].astype(F32)).astype(BF16)

            @pl.when(z == 0)
            def _():
                for k in range(own_count):
                    to_right[o, k] = placed(o, k).astype(BF16)

            back_right(o).start()

        o2 = z - (nz - 1) + t

        @pl.when((o2 >= 0) & (o2 < z))
        def _():
            @pl.when(z < nz - 1)
            def _():
                back_left(o2).wait_recv()
                for k in range(own_count):
                    to_left[o2, k] = (placed(o2, k) + from_right[o2, k].astype(F32)).astype(BF16)

            @pl.when(z == nz - 1)
            def _():
                for k in range(own_count):
                    to_left[o2, k] = placed(o2, k).astype(BF16)

            back_left(o2).start()

    def step(s, carry):
        @pl.when(s < nz)
        def _():
            fwd_step(s)

        @pl.when(s == 1)
        def _():
            for d in range(1, nx):
                x_back(d).wait_recv()
            for k in range(own_count):
                far_out[k] = placed_col(1 - zh, 1, k).astype(BF16)
            back_far.start()

        @pl.when(s == LAG)
        def _():
            for d in range(1, ny):
                y_back(d).wait_recv()

        @pl.when(s >= LAG)
        def _():
            bwd_step(s - LAG)

        @pl.when(s == 3)
        def _():
            blocks_far.wait_recv()
            forward_col(1, far)

        if with_sum:
            for k in range(1, len(ar)):
                @pl.when(s == k)
                def _(k=k):
                    ar[k]()
        return carry

    lax.fori_loop(1, max(nz + LAG - 1, 10), step, 0)

    for k in range(own_count):
        back[k] = placed(z, k) + placed_col(zh, 0, k)

    @pl.when(z > 0)
    def _():
        back_right(z).wait_recv()
        for k in range(own_count):
            back[k] += from_left[z, k].astype(F32)

    @pl.when(z < nz - 1)
    def _():
        back_left(z).wait_recv()
        for k in range(own_count):
            back[k] += from_right[z, k].astype(F32)

    back_far.wait_recv()
    for k in range(own_count):
        back[k] += far_in[k].astype(F32)

    def arrive(src, carry):
        for d in range(1, ny):
            y_in(d, src).wait_recv()
            y_out(d, src).wait_send()

        @pl.when((src <= z) & (z < nz - 1))
        def _():
            right(src).wait_send()

        @pl.when((src >= z) & (z > 0))
        def _():
            left(src).wait_send()

        @pl.when(src > z)
        def _():
            back_right(src).wait_send()

        @pl.when(src < z)
        def _():
            back_left(src).wait_send()

        return carry

    lax.fori_loop(0, nz, arrive, 0)
    for d in range(1, nx):
        for s in range(2):
            c_in(d, s).wait_recv()
            c_out(d, s).wait_send()
        x_back(d).wait_send()
    for d in range(1, ny):
        y_back(d).wait_send()
    for d in range(1, nz):
        idx_copy(d).wait_send()
    idx_far.wait_send()
    blocks_far.wait_send()
    back_far.wait_send()


def sum_stages(split, gr, gout, refs, where, remote):
    ny, nz, nx = split["y"], split["z"], split["xc"] // 2
    r, c, y, z, zh, xc = where
    core, x = lax.rem(xc, 2), lax.div(xc, 2)
    (a1, v1, a2, v2, a3, a4, a5, v5, w1, w2, s1, r1, s2, r2, s3, r3, s4, r4, s5, r5,
     s6, r6, s7, r7, s8, r8) = refs
    half = gr.shape[0] // 2
    part = half // nx
    piece = part // ny
    sx = split["xc"]
    partner = (1 - zh) * sx + xc
    other = zh * sx + x * 2 + (1 - core)

    def xcol(d):
        xx = lax.rem(x + d, nx)
        return xx, zh * sx + xx * 2 + core

    def yrow(d):
        yy = lax.rem(y + d, ny)
        return yy, yy * nz + z

    def rows_of(i, n):
        return pl.ds(pl.multiple_of(i * n, n), n)

    c1 = remote(gr.at[rows_of(1 - core, half)], a1, s1.at[0], r1.at[0], r, other)

    def c2(d):
        xx, col = xcol(d)
        return remote(v1.at[rows_of(xx, part)], a2.at[(nx - d) % nx], s2.at[d], r2.at[(nx - d) % nx], r, col)

    def c3(d):
        yy, row = yrow(d)
        return remote(v2.at[rows_of(yy, piece)], a3.at[(ny - d) % ny], s3.at[d], r3.at[(ny - d) % ny], row, c)

    def c4(d, slot):
        zz = lax.rem(z + d, nz)
        to = z if slot is None else zz
        return remote(a4.at[z], a4.at[to], s4.at[d], r4.at[to], y * nz + zz, c)

    c5 = remote(v5.at[0], a5, s5.at[0], r5.at[0], r, partner)

    def c6(d, slot):
        yy, row = yrow(d)
        to = y if slot is None else yy
        here = w1.at[rows_of(y, piece)]
        return remote(here, w1.at[rows_of(to, piece)], s6.at[d], r6.at[to], row, c)

    def c7(d, slot):
        xx, col = xcol(d)
        to = x if slot is None else xx
        here = w2.at[rows_of(x, part)]
        return remote(here, w2.at[rows_of(to, part)], s7.at[d], r7.at[to], r, col)

    c8 = remote(w2, gout.at[rows_of(core, half)], s8.at[0], r8.at[0], r, other)
    c8_in = remote(w2, gout.at[rows_of(1 - core, half)], s8.at[0], r8.at[0], r, other)

    def t0():
        c1.start()

    def t1():
        c1.wait_recv()
        v1[...] = gr[rows_of(core, half)] + a1[...]
        for d in range(1, nx):
            c2(d).start()

    def t2():
        total = v1[rows_of(x, part)]
        for d in range(1, nx):
            c2(d).wait_recv()
        for d in range(1, nx):
            total = total + a2[d]
        v2[...] = total
        for d in range(1, ny):
            c3(d).start()

    def t3():
        total = v2[rows_of(y, piece)]
        for d in range(1, ny):
            c3(d).wait_recv()
        for d in range(1, ny):
            total = total + a3[d]
        a4[z] = total
        for d in range(1, nz):
            c4(d, None).start()

    def t4():
        for d in range(1, nz):
            c4(d, 1).wait_recv()
        total = a4[0]
        for i in range(1, nz):
            total = total + a4[i]
        v5[0] = total
        c5.start()

    def t5():
        c5.wait_recv()
        w1[rows_of(y, piece)] = v5[0] + a5[...]
        for d in range(1, ny):
            c6(d, None).start()

    def t6():
        for d in range(1, ny):
            c6(d, 1).wait_recv()
        w2[rows_of(x, part)] = w1[...]
        for d in range(1, nx):
            c7(d, None).start()

    def t7():
        for d in range(1, nx):
            c7(d, 1).wait_recv()
        gout[rows_of(core, half)] = w2[...]
        c8.start()

    def t8():
        c8_in.wait_recv()
        c1.wait_send()
        for d in range(1, nx):
            c2(d).wait_send()
            c7(d, None).wait_send()
        for d in range(1, ny):
            c3(d).wait_send()
            c6(d, None).wait_send()
        for d in range(1, nz):
            c4(d, None).wait_send()
        c5.wait_send()
        c8.wait_send()

    return [t0, t1, t2, t3, t4, t5, t6, t7, t8]


def exchange(split, own, gsend, idx, grads, collective_id):
    ny, nz, nh, nx = split["y"], split["z"], split["zh"], split["xc"]
    own_count, rows, feat = own.shape
    size = own_count + ny * nz + nh * nx
    blocks = (own_count, rows, feat)
    one = (rows, feat)
    dma = pltpu.SemaphoreType.DMA
    scratch = [
        pltpu.VMEM((nz,) + blocks, BF16),
        pltpu.VMEM(blocks, BF16),
        pltpu.VMEM((nz + 1, 8, 128), jnp.int32),
        pltpu.VMEM((ny, nz, 8, 128), F32),
        pltpu.VMEM((nx, 2, 8, 128), F32),
        pltpu.VMEM((ny, nz) + one, BF16),
        pltpu.VMEM((nx, 2) + one, BF16),
        pltpu.VMEM((ny, nz) + one, BF16),
        pltpu.VMEM((nx, nh) + one, BF16),
        pltpu.VMEM((nz,) + blocks, BF16),
        pltpu.VMEM((nz,) + blocks, BF16),
        pltpu.VMEM((nz,) + blocks, BF16),
        pltpu.VMEM((nz,) + blocks, BF16),
        pltpu.VMEM(blocks, BF16),
        pltpu.VMEM(blocks, BF16),
        dma((nz,)), dma((nz + 1,)), dma((nz,)), dma((nz,)), dma((nz,)), dma((2,)), dma((2,)),
        dma((ny, nz)), dma((ny, nz)), dma((nx, 2)), dma((nx, 2)),
        dma((ny,)), dma((ny,)), dma((nx,)), dma((nx,)),
        dma((nz,)), dma((nz,)), dma((nz,)), dma((nz,)),
    ]
    out_shape = [
        jax.ShapeDtypeStruct((size, rows, feat), BF16),
        jax.ShapeDtypeStruct(blocks, F32),
    ]
    args = [own, gsend, idx]
    if grads is not None:
        args.append(grads)
        out_shape.append(jax.ShapeDtypeStruct(grads.shape, F32))
        half = grads.shape[0] // 2
        cx = nx // 2
        part = half // cx
        piece = part // ny
        scratch += [
            pltpu.VMEM((half, 128), F32),
            pltpu.VMEM((half, 128), F32),
            pltpu.VMEM((cx, part, 128), F32),
            pltpu.VMEM((part, 128), F32),
            pltpu.VMEM((ny, piece, 128), F32),
            pltpu.VMEM((nz, piece, 128), F32),
            pltpu.VMEM((piece, 128), F32),
            pltpu.VMEM((1, piece, 128), F32),
            pltpu.VMEM((part, 128), F32),
            pltpu.VMEM((half, 128), F32),
            dma((1,)), dma((1,)), dma((cx,)), dma((cx,)), dma((ny,)), dma((ny,)),
            dma((nz,)), dma((nz,)), dma((1,)), dma((1,)), dma((ny,)), dma((ny,)),
            dma((cx,)), dma((cx,)), dma((1,)), dma((1,)),
        ]
    vmem = pl.BlockSpec(memory_space=pltpu.VMEM)
    return pl.pallas_call(
        functools.partial(exchange_kernel, split, grads is not None),
        out_shape=out_shape,
        in_specs=[vmem] * len(args),
        out_specs=[vmem] * len(out_shape),
        scratch_shapes=scratch,
        compiler_params=pltpu.CompilerParams(
            collective_id=collective_id, has_side_effects=True, vmem_limit_bytes=LIMIT
        ),
    )(*args)


def grad_slot(split, own_count, t):
    nh, nx = split["zh"], split["xc"]
    first = own_count + split["y"] * split["z"]
    q = t - first
    return jnp.where(t < first, t, first + nh * lax.rem(q, nx) + lax.div(q, nx))


def spread(split, own_count, adj, dst, src, q, grad):
    @pl.loop(0, grad.shape[0])
    def _(i):
        grad[i] = jnp.zeros(grad.shape[1:], F32)

    def one(e, carry):
        grad[grad_slot(split, own_count, src[e])] += dot_at(adj[e], q[dst[e]])
        return carry

    lax.fori_loop(0, adj.shape[0], one, 0, unroll=4)


def gather(adj, dst, src, table, acc):
    def one(e, carry):
        acc[dst[e]] += dot(adj[e], table[src[e]])
        return carry

    lax.fori_loop(0, adj.shape[0], one, 0, unroll=4)


def send_out(own_count, grad, gsend):
    @pl.loop(0, gsend.shape[0])
    def _(i):
        gsend[i] = grad[own_count + i].astype(BF16)


def first_kernel(split, dst, src, adj, cot, deg, u_own, gsend, grad, q):
    own_count = cot.shape[0]
    deg[...] = jnp.ones_like(deg)
    ones = jnp.ones(adj.shape[1:], BF16)

    def one(e, carry):
        deg[dst[e]] += dot(adj[e], ones)
        return carry

    lax.fori_loop(0, adj.shape[0], one, 0, unroll=4)
    for b in range(own_count):
        q[b] = (cot[b].astype(F32) / deg[b]).astype(BF16)
    spread(split, own_count, adj, dst, src, q, grad)
    for b in range(own_count):
        u_own[b] = grad[b] + q[b].astype(F32)
    send_out(own_count, grad, gsend)


def middle_kernel(split, scale, dst, src, adj, feat, table, deg, u_own, u_back, cot,
                  ws1, wn1, ws2, wn2, hidden, base, gsend, grads, acc, grad, q):
    own_count, rows, width = feat.shape
    for b in range(own_count):
        acc[b] = feat[b].astype(F32)
    gather(adj, dst, src, table, acc)
    g1, g2, g3, g4 = 0.0, 0.0, 0.0, 0.0
    for b in range(own_count):
        mean = (acc[b] / deg[b]).astype(BF16)
        pre = dot(feat[b], ws1[...]) + dot(mean, wn1[...])
        s = 1.0 / (1.0 + jnp.exp(-pre))
        hid = (pre * s).astype(BF16)
        hidden[b] = hid
        u = u_own[b] + u_back[b]
        hi = u.astype(BF16)
        lo = (u - hi.astype(F32)).astype(BF16)
        dh = dot_bt(cot[b], ws2[...]) + (dot_bt(hi, wn2[...]) + dot_bt(lo, wn2[...]))
        dpre = (dh * (s * (1.0 + pre * (1.0 - s)))).astype(BF16)
        qb = (dot_bt(dpre, wn1[...]) / deg[b]).astype(BF16)
        q[b] = qb
        base[b] = dot_bt(dpre, ws1[...]) + qb.astype(F32)
        g1 = g1 + dot_at(feat[b], dpre)
        g2 = g2 + dot_at(mean, dpre)
        g3 = g3 + dot_at(hid, cot[b])
        g4 = g4 + (dot_at(hid, hi) + dot_at(hid, lo))
    for i, g in enumerate((g1, g2, g3, g4)):
        grads[pl.ds(i * width, width), :] = g * scale
    spread(split, own_count, adj, dst, src, q, grad)
    for b in range(own_count):
        base[b] += grad[b]
    send_out(own_count, grad, gsend)


def last_kernel(dst, src, adj, hidden, table, deg, base, back, ws2, wn2, out, grad_in, acc):
    own_count = hidden.shape[0]
    for b in range(own_count):
        acc[b] = hidden[b].astype(F32)
    gather(adj, dst, src, table, acc)
    for b in range(own_count):
        mean = (acc[b] / deg[b]).astype(BF16)
        out[b] = (dot(hidden[b], ws2[...]) + dot(mean, wn2[...])).astype(BF16)
        grad_in[b] = base[b] + back[b]


def on_device(body, edges, args, out_shape, scratch):
    smem = pl.BlockSpec(memory_space=pltpu.SMEM)
    vmem = pl.BlockSpec(memory_space=pltpu.VMEM)
    return pl.pallas_call(
        body,
        out_shape=out_shape,
        in_specs=[smem] * len(edges) + [vmem] * len(args),
        out_specs=[vmem] * len(out_shape),
        scratch_shapes=scratch,
        compiler_params=pltpu.CompilerParams(vmem_limit_bytes=LIMIT),
    )(*edges, *args)


def local(
    split,
    nodes,
    features,
    adjacency,
    edge_dst,
    edge_src,
    send_row,
    send_col,
    w_self1,
    w_neigh1,
    w_self2,
    w_neigh2,
    cotangent,
):
    own = features[0, 0]
    adj = adjacency[0, 0]
    edges = (edge_dst[0, 0], edge_src[0, 0])
    cot = cotangent[0, 0]
    own_count, rows, width = own.shape
    lists = jnp.concatenate([send_row.reshape(-1), send_col.reshape(-1)])
    remote_count = lists.size
    idx = jnp.broadcast_to(jnp.pad(lists, (0, 128 - remote_count))[None, :], (8, 128))
    size = own_count + remote_count
    blocks = (own_count, rows, width)
    full = jax.ShapeDtypeStruct(blocks, F32)
    half = jax.ShapeDtypeStruct(blocks, BF16)
    sends = jax.ShapeDtypeStruct((remote_count, rows, width), BF16)
    grad = pltpu.VMEM((size, rows, width), F32)
    acc = pltpu.VMEM(blocks, F32)
    q = pltpu.VMEM(blocks, BF16)
    deg, u_own, gsend = on_device(
        functools.partial(first_kernel, split), edges, (adj, cot), [full, full, sends], [grad, q]
    )
    table, u_back = exchange(split, own, gsend, idx, None, 0)
    weights = jax.ShapeDtypeStruct((4 * width, width), F32)
    hidden, base, gsend, grads = on_device(
        functools.partial(middle_kernel, split, 1.0 / math.sqrt(nodes)),
        edges,
        (adj, own, table, deg, u_own, u_back, cot, w_self1, w_neigh1, w_self2, w_neigh2),
        [half, full, sends, weights],
        [acc, grad, q],
    )
    table, back, grads = exchange(split, hidden, gsend, idx, grads, 1)
    out, grad_in = on_device(
        last_kernel,
        edges,
        (adj, hidden, table, deg, base, back, w_self2, w_neigh2),
        [half, full],
        [acc],
    )
    g = grads.reshape(4, width, width)
    return (
        out.reshape(features.shape),
        grad_in.reshape(features.shape),
        g[0],
        g[1],
        g[2],
        g[3],
    )


def solution(mesh):
    blocked = P("row", "col", None, None, None)
    placed = (
        blocked,
        blocked,
        P("row", "col", None),
        P("row", "col", None),
        P("row", "col", None, None),
        P("row", "col", None, None),
        P(),
        P(),
        P(),
        P(),
        blocked,
    )

    def whole(*args):
        shape = args[0].shape
        nodes = shape[0] * shape[1] * shape[2] * shape[3]
        return jax.shard_map(
            functools.partial(local, SPLIT, nodes),
            mesh=mesh,
            in_specs=placed,
            out_specs=(blocked, blocked, P(), P(), P(), P()),
            check_vma=False,
        )(*args)

    return whole
```

time: 991 us -> 184 us (0.19)
  the two profiles are of different devices: /device:TPU:1 before, /device:TPU:32 now
where the time goes in v1:
time: 184 us
  Pallas kernels  178 us (97%)
  local copies, waits for them, and re-layouts  5.02 us (3%)
    pallas_call x2, Pallas kernels, exchange(): pl.pallas_call(functools.partial(exchange_kernel, split, grads is not Non...  165 us
    pallas_call x3, Pallas kernels, on_device(): pl.pallas_call(body, out_shape=out_shape, in_specs=[smem] * len(edges) +...  12.3 us
    unnamed x20, local copies, waits for them, and re-layouts  4.31 us

profile of v1, /device:TPU:32, one launch (start us, length us, event | category | flops | bytes accessed | tf_op | source)
XLA Modules:
  0.0 184.0 jit_solution(14624659102613646329)
XLA Ops:
  0.6 0.7 pad_add_fusion
  1.4 0.0 copy-start
  1.4 1.2 copy-done
  2.6 0.0 copy-start.2
  2.6 0.9 copy-done.2
  3.5 0.0 copy-start.8
  3.5 0.7 copy-done.8
  4.1 0.0 copy-start.9
  4.1 0.7 copy-done.9
  4.8 0.0 copy-start.1
  4.8 0.0 copy-start.4
  4.8 0.0 copy-start.5
  4.8 0.0 copy-start.6
  4.8 0.0 copy-start.7
  4.8 4.1 %shard_map.154 = (f32[4,128,128]{2,1,0:T(8,128)S(1)}, f32[4,128,128]{2,1,0:T(8,128)S(1)}, bf16[48,128,128]{2,1,0:T(8,128)(2,1)S(1)}) custom-call(s32[28]{0:T(128)S(1)} %bitcast.16, s32[28]{0:T(128)S(1)} %bitcast.19, bf16[28,128,128]{2,1,0:T(8,128)(2,1)S(1)} %bitcast.9, bf16[4,128,128]{2,1,0:T(8,128)(2,1)S(1)} %bitcast.12), custom_call_target="tpu_custom_call" | custom-call | tf_op jit(solution)/shard_map/pallas_call | solution.py:675
  8.9 0.0 copy-start.3
  8.9 0.9 copy-done.3
  9.8 82.3 %shard_map.155 = (bf16[52,128,128]{2,1,0:T(8,128)(2,1)S(1)}, f32[4,128,128]{2,1,0:T(8,128)S(1)}) custom-call(bf16[4,128,128]{2,1,0:T(8,128)(2,1)S(1)} %bitcast.14, bf16[48,128,128]{2,1,0:T(8,128)(2,1)S(1)} %get-tuple-element.20.refs_1_, s32[8,128]{1,0:T(8,128)S(1)} %broadcast_in_dim.2.refs_2_), custom_call_target="tpu_custom_call" | custom-call | tf_op jit(solution)/shard_map/pallas_call | solution.py:565
  92.2 0.0 copy-done.1
  92.2 0.0 copy-done.4
  92.2 0.0 copy-done.5
  92.2 0.0 copy-done.6
  92.2 0.0 copy-done.7
  92.2 5.5 %shard_map.156 = (bf16[4,128,128]{2,1,0:T(8,128)(2,1)S(1)}, f32[4,128,128]{2,1,0:T(8,128)S(1)}, bf16[48,128,128]{2,1,0:T(8,128)(2,1)S(1)}, f32[512,128]{1,0:T(8,128)S(1)}) custom-call(s32[28]{0:T(128)S(1)} %bitcast.17, s32[28]{0:T(128)S(1)} %bitcast.20, bf16[28,128,128]{2,1,0:T(8,128)(2,1)S(1)} %bitcast.10, bf16[4,128,128]{2,1,0:T(8,128)(2,1)S(1)} %bitcast.15, ...), custom_call_target="tpu_custom_call" | custom-call | tf_op jit(solution)/shard_map/pallas_call | solution.py:675
  97.7 82.9 %shard_map.157 = (bf16[52,128,128]{2,1,0:T(8,128)(2,1)S(1)}, f32[4,128,128]{2,1,0:T(8,128)S(1)}, f32[512,128]{1,0:T(8,128)S(1)}) custom-call(bf16[4,128,128]{2,1,0:T(8,128)(2,1)S(1)} %get-tuple-element.25.refs_0_.hidden, bf16[48,128,128]{2,1,0:T(8,128)(2,1)S(1)} %get-tuple-element.26.refs_1_, s32[8,128]{1,0:T(8,128)S(1)} %broadcast_in_dim.2.refs_2_, ...), custom_call_target="tpu_custom_call" | custom-call | tf_op jit(solution)/shard_map/pallas_call | solution.py:565
  180.6 2.7 %shard_map.158 = (bf16[4,128,128]{2,1,0:T(8,128)(2,1)}, f32[4,128,128]{2,1,0:T(8,128)}) custom-call(s32[28]{0:T(128)S(1)} %bitcast.18, s32[28]{0:T(128)S(1)} %bitcast.21, bf16[28,128,128]{2,1,0:T(8,128)(2,1)S(1)} %bitcast.11, bf16[4,128,128]{2,1,0:T(8,128)(2,1)S(1)} %get-tuple-element.25.refs_0_.hidden, bf16[52,128,128]{2,1,0:T(8,128)(2,1)S(1)} %get-tuple-element.28.table, ...), custom_call_target="tpu_custom_call" | custom-call | tf_op jit(solution)/shard_map/pallas_call | solution.py:675
  183.3 0.7 fusion
  (2 shorter events, 0.0 us)
Async XLA Ops:
  1.4 1.2 copy-start
  2.6 0.9 copy-start.2
  3.5 0.7 copy-start.8
  4.1 0.7 copy-start.9
  4.8 87.4 %copy-start.1 = (bf16[1,1,28,128,128]{4,3,2,1,0:T(8,128)(2,1)S(1)}, bf16[1,1,28,128,128]{4,3,2,1,0:T(8,128)(2,1)}, u32[]{:S(2)}) copy-start(bf16[1,1,28,128,128]{4,3,2,1,0:T(8,128)(2,1)} %param.12) | copy-start | bytes 2752516
  4.8 87.4 %copy-start.4 = (bf16[128,128]{1,0:T(8,128)(2,1)S(1)}, bf16[128,128]{1,0:T(8,128)(2,1)}, u32[]{:S(2)}) copy-start(bf16[128,128]{1,0:T(8,128)(2,1)} %ws2.3) | copy-start | bytes 98308
  4.8 87.4 %copy-start.5 = (bf16[128,128]{1,0:T(8,128)(2,1)S(1)}, bf16[128,128]{1,0:T(8,128)(2,1)}, u32[]{:S(2)}) copy-start(bf16[128,128]{1,0:T(8,128)(2,1)} %wn2.3) | copy-start | bytes 98308
  4.8 87.4 %copy-start.6 = (bf16[128,128]{1,0:T(8,128)(2,1)S(1)}, bf16[128,128]{1,0:T(8,128)(2,1)}, u32[]{:S(2)}) copy-start(bf16[128,128]{1,0:T(8,128)(2,1)} %ws1.1) | copy-start | bytes 98308
  4.8 87.4 %copy-start.7 = (bf16[128,128]{1,0:T(8,128)(2,1)S(1)}, bf16[128,128]{1,0:T(8,128)(2,1)}, u32[]{:S(2)}) copy-start(bf16[128,128]{1,0:T(8,128)(2,1)} %wn1.1) | copy-start | bytes 98308
  8.9 0.9 copy-start.3

commit v2 on v1

--- a/solution.py
+++ b/solution.py
@@ -13,7 +13,8 @@
 F32 = jnp.float32
 LIMIT = 44 * 1024 * 1024
 SPLIT = {"y": 4, "z": 8, "zh": 2, "xc": 8}
-LAG = 3
+LAG = 2
+CUT = 2
 
 
 def dot(a, b):
@@ -28,9 +29,9 @@
     return lax.dot_general(a, b, (((0,), (0,)), ((), ())), preferred_element_type=F32)
 
 
-def exchange_kernel(split, with_sum, *refs):
+def exchange_kernel(split, lag, cut, with_sum, *refs):
     ny, nz, nh, nx = split["y"], split["z"], split["zh"], split["xc"]
-    nrow, ncol = ny * nz, nh * nx
+    nrow, ring = ny * nz, nh * nz
     refs = list(refs)
     own, gsend, idx = refs[:3]
     del refs[:3]
@@ -40,30 +41,41 @@
     del refs[:2]
     if with_sum:
         gout = refs.pop(0)
-    (chain, far, tiles, pick_row, pick_col, stage_y, stage_c, land_y, land_c, from_left, from_right,
-     to_right, to_left, far_out, far_in) = refs[:15]
-    (i_s, i_r, f_r, f_sr, f_sl, h_s, h_r, yf_s, yf_r, cf_s, cf_r, yb_s, yb_r, cb_s, cb_r,
-     b_rl, b_rr, b_sr, b_sl) = refs[15:34]
+    (chain, tiles, pick_row, pick_col, stage_y, stage_c, land_y, land_c, in_right, in_left,
+     out_left, out_right, ready, far_out) = refs[:14]
+    (i_s, i_r, f_r, f_sr, f_sl, yf_s, yf_r, cf_s, cf_r, yb_s, yb_r, cb_s, cb_r,
+     br_r, bl_r, b_sl, b_sr) = refs[14:31]
     own_count, rows, feat = own.shape
+    per = own_count // cut
 
     r = lax.axis_index("row")
     c = lax.axis_index("col")
     y, z = lax.div(r, nz), lax.rem(r, nz)
     zh, xc = lax.div(c, nx), lax.rem(c, nx)
+    g = zh * nz + z
+    partner = (1 - zh) * nx + xc
 
     def y_peer(d):
         return lax.rem(y + d, ny)
 
     def x_peer(d):
         return lax.rem(xc + d, nx)
+
+    def at_ring(pos):
+        pos = lax.rem(pos + ring, ring)
+        return y * nz + lax.rem(pos, nz), lax.div(pos, nz) * nx + xc
+
+    def reach_right(src):
+        return jnp.where(src < nz // 2, nz, nz - 1 - src)
+
+    def reach_left(src):
+        return jnp.where(src < nz // 2, src, nz)
 
     def remote(src, dst, ssem, rsem, row, col):
         return pltpu.make_async_remote_copy(
             src_ref=src, dst_ref=dst, send_sem=ssem, recv_sem=rsem,
             device_id=(row, col), device_id_type=MESH,
         )
-
-    partner = (1 - zh) * nx + xc
 
     barrier = pltpu.get_barrier_semaphore()
 
@@ -77,7 +89,25 @@
     greet(r, partner)
     for d in range(1, nx):
         greet(r, zh * nx + x_peer(d))
-    pl.semaphore_wait(barrier, (ny - 1) + (nz - 1) + 1 + (nx - 1))
+    at_end = (z == 0) | (z == nz - 1)
+
+    @pl.when(z == 0)
+    def _():
+        greet(*at_ring(g - 1))
+
+    @pl.when(z == nz - 1)
+    def _():
+        greet(*at_ring(g + 1))
+
+    met = (ny - 1) + (nz - 1) + 1 + (nx - 1)
+
+    @pl.when(at_end)
+    def _():
+        pl.semaphore_wait(barrier, met + 1)
+
+    @pl.when(jnp.logical_not(at_end))
+    def _():
+        pl.semaphore_wait(barrier, met)
 
     def idx_copy(d):
         zz = lax.rem(z + d, nz)
@@ -88,25 +118,30 @@
         return remote(idx, tiles.at[zz], i_s.at[d], i_r.at[zz], y * nz + zz, c)
 
     idx_far = remote(idx, tiles.at[nz], i_s.at[0], i_r.at[nz], r, partner)
-    blocks_far = remote(own, far, h_s.at[0], h_r.at[0], r, partner)
-    back_far = remote(far_out, far_in, h_s.at[1], h_r.at[1], r, partner)
-
-    def right(src):
-        return remote(chain.at[src], chain.at[src], f_sr.at[src], f_r.at[src], r + 1, c)
-
-    def left(src):
-        return remote(chain.at[src], chain.at[src], f_sl.at[src], f_r.at[src], r - 1, c)
-
-    def back_right(o):
-        return remote(to_right.at[o], from_left.at[o], b_sr.at[o], b_rl.at[o], r + 1, c)
-
-    def back_left(o):
-        return remote(to_left.at[o], from_right.at[o], b_sl.at[o], b_rr.at[o], r - 1, c)
-
-    def y_back(d):
+
+    def part(ref, slot, ch):
+        return ref.at[slot, pl.ds(ch * per, per)]
+
+    def right(src, ch):
+        ref = part(chain, src, ch)
+        return remote(ref, ref, f_sr.at[src, ch], f_r.at[src, ch], *at_ring(g + 1))
+
+    def left(src, ch):
+        ref = part(chain, src, ch)
+        return remote(ref, ref, f_sl.at[src, ch], f_r.at[src, ch], *at_ring(g - 1))
+
+    def back_left(o, ch, buf):
+        return remote(part(buf, o, ch), part(in_right, o, ch), b_sl.at[o, ch], br_r.at[o, ch],
+                      *at_ring(g - 1))
+
+    def back_right(o, ch, buf):
+        return remote(part(buf, o, ch), part(in_left, o, ch), b_sr.at[o, ch], bl_r.at[o, ch],
+                      *at_ring(g + 1))
+
+    def y_back(d, o):
         yy = y_peer(d)
-        return remote(gsend.at[pl.ds(yy * nz, nz)], land_y.at[(ny - d) % ny],
-                      yb_s.at[d], yb_r.at[(ny - d) % ny], yy * nz + z, c)
+        return remote(gsend.at[yy * nz + o], land_y.at[(ny - d) % ny, o],
+                      yb_s.at[d, o], yb_r.at[(ny - d) % ny, o], yy * nz + z, c)
 
     def x_back(d):
         xx = x_peer(d)
@@ -138,25 +173,33 @@
     for d in range(1, nz):
         idx_copy(d).start()
     idx_far.start()
-    chain[z] = own[...]
+    chain[g] = own[...]
     tiles[z] = idx[...]
-
-    @pl.when(z < nz - 1)
-    def _():
-        right(z).start()
-
-    @pl.when(z > 0)
-    def _():
-        left(z).start()
-
-    for d in range(1, ny):
-        y_back(d).start()
+    for ch in range(cut):
+        @pl.when(reach_right(z) > 0)
+        def _(ch=ch):
+            right(g, ch).start()
+
+        @pl.when(reach_left(z) > 0)
+        def _(ch=ch):
+            left(g, ch).start()
+
     for d in range(1, nx):
         x_back(d).start()
-    blocks_far.start()
+
+    def first_y(i, carry):
+        away = nz - 1 - i
+        for o, ok in ((z - away, away <= z), (z + away, (away > 0) & (z + away < nz))):
+            @pl.when(ok)
+            def _(o=o):
+                for d in range(1, ny):
+                    y_back(d, o).start()
+        return carry
+
+    lax.fori_loop(0, nz, first_y, 0)
 
     if with_sum:
-        ar = sum_stages(split, gr, gout, refs[34:], (r, c, y, z, zh, xc), remote)
+        ar = sum_stages(split, gr, gout, refs[31:], (r, c, y, z, zh, xc), remote)
         ar[0]()
 
     table[pl.ds(0, own_count)] = own[...]
@@ -177,27 +220,29 @@
         hot = jnp.where(lane == nrow + zh * nx + x_peer(d), 1.0, 0.0).astype(BF16)
         pick_col[d] = dot(pair, hot).reshape(2, 8, 128)
 
-    def choose(which, blocks):
-        row = which[0:1, :]
+    def hot_row(which, k):
+        return jnp.where(which[0:1, :] == k, 1.0, 0.0)
+
+    def choose(which, slot):
         total = None
         for k in range(own_count):
-            term = blocks[k].astype(F32) * jnp.where(row == k, 1.0, 0.0)
+            term = chain[slot, k] * hot_row(which, k).astype(BF16)
             total = term if total is None else total + term
-        return total.astype(BF16)
+        return total
 
     def forward(src):
-        blocks = chain.at[src]
+        slot = zh * nz + src
         for d in range(ny):
-            chosen = choose(pick_row[d, src], blocks)
+            chosen = choose(pick_row[d, src], slot)
             if d == 0:
                 table[own_count + y * nz + src] = chosen
             else:
                 stage_y[d, src] = chosen
                 y_out(d, src).start()
 
-    def forward_col(s, blocks):
+    def forward_col(s, slot):
         for d in range(nx):
-            chosen = choose(pick_col[d, s], blocks)
+            chosen = choose(pick_col[d, s], slot)
             if d == 0:
                 table[col_slot(s, xc)] = chosen
             else:
@@ -207,109 +252,117 @@
     def placed(o, k):
         total = None
         for d in range(ny):
-            hot = jnp.where(pick_row[d, o][0:1, :] == k, 1.0, 0.0)
-            term = land_y[d, o].astype(F32) * hot
+            term = land_y[d, o].astype(F32) * hot_row(pick_row[d, o], k)
             total = term if total is None else total + term
         return total
 
     def placed_col(half, s, k):
         total = None
         for d in range(nx):
-            hot = jnp.where(pick_col[d, s][0:1, :] == k, 1.0, 0.0)
-            term = land_c[d, half].astype(F32) * hot
+            term = land_c[d, half].astype(F32) * hot_row(pick_col[d, s], k)
             total = term if total is None else total + term
         return total
 
+    def y_arrived(o):
+        for d in range(1, ny):
+            y_back(d, o).wait_recv()
+
     forward(z)
-    forward_col(0, own)
-
-    def fwd_step(s):
-        src = z - s
-
-        @pl.when(src >= 0)
+
+    def coming(s, way):
+        src = lax.rem(g + ring - s if way == 0 else g + s, ring)
+        low = lax.rem(src, nz)
+        reach = reach_right(low) if way == 0 else reach_left(low)
+        return src, low, (s >= 1) & (s <= nz) & (s <= reach), s < reach, lax.div(src, nz) == zh
+
+    def fwd_step(s, ch):
+        for way, copy in ((0, right), (1, left)):
+            src, low, comes, goes_on, mine = coming(s, way)
+
+            @pl.when(comes)
+            def _():
+                copy(src, ch).wait_recv()
+
+            @pl.when(comes & goes_on)
+            def _():
+                copy(src, ch).start()
+
+    def deliver(s):
+        for way in range(2):
+            src, low, comes, goes_on, mine = coming(s, way)
+
+            @pl.when(comes & mine)
+            def _():
+                forward(low)
+
+        @pl.when(s == nz)
         def _():
-            right(src).wait_recv()
-
-            @pl.when(z < nz - 1)
-            def _():
-                right(src).start()
-
-            forward(src)
-
-        src2 = z + s
-
-        @pl.when(src2 < nz)
-        def _():
-            left(src2).wait_recv()
-
-            @pl.when(z > 0)
-            def _():
-                left(src2).start()
-
-            forward(src2)
-
-    def bwd_step(t):
-        o = nz - 1 + z - t
-
-        @pl.when((o > z) & (o < nz))
-        def _():
-            @pl.when(z > 0)
-            def _():
-                back_right(o).wait_recv()
+            forward_col(1, lax.rem(g + nz, ring))
+
+    def prepare(t):
+        for way in range(2):
+            o, low, comes, has_in, mine = coming(nz - t, way)
+
+            @pl.when(comes & mine & (t >= 0))
+            def _():
+                y_arrived(low)
                 for k in range(own_count):
-                    to_right[o, k] = (placed(o, k) + from_left[o, k].astype(F32)).astype(BF16)
-
-            @pl.when(z == 0)
-            def _():
-                for k in range(own_count):
-                    to_right[o, k] = placed(o, k).astype(BF16)
-
-            back_right(o).start()
-
-        o2 = z - (nz - 1) + t
-
-        @pl.when((o2 >= 0) & (o2 < z))
-        def _():
-            @pl.when(z < nz - 1)
-            def _():
-                back_left(o2).wait_recv()
-                for k in range(own_count):
-                    to_left[o2, k] = (placed(o2, k) + from_right[o2, k].astype(F32)).astype(BF16)
-
-            @pl.when(z == nz - 1)
-            def _():
-                for k in range(own_count):
-                    to_left[o2, k] = placed(o2, k).astype(BF16)
-
-            back_left(o2).start()
-
-    def step(s, carry):
-        @pl.when(s < nz)
-        def _():
-            fwd_step(s)
-
-        @pl.when(s == 1)
+                    ready[way, k] = placed(low, k)
+
+        @pl.when(t == 0)
         def _():
             for d in range(1, nx):
                 x_back(d).wait_recv()
             for k in range(own_count):
-                far_out[k] = placed_col(1 - zh, 1, k).astype(BF16)
-            back_far.start()
-
-        @pl.when(s == LAG)
+                far_out[0, k] = placed_col(1 - zh, 1, k).astype(BF16)
+
+    def far_copy(way, o, ch):
+        if way == 0:
+            return remote(part(far_out, 0, ch), part(in_right, o, ch), b_sl.at[o, ch], br_r.at[o, ch],
+                          *at_ring(g - 1))
+        return remote(part(far_out, 0, ch), part(in_left, o, ch), b_sr.at[o, ch], bl_r.at[o, ch],
+                      *at_ring(g + 1))
+
+    def bwd_step(t, ch):
+        for way, copy, got, out in ((0, back_left, in_right, out_left), (1, back_right, in_left, out_right)):
+            o, low, comes, has_in, mine = coming(nz - t, way)
+            sends = comes & (t >= 0)
+
+            @pl.when(sends & has_in)
+            def _():
+                copy(o, ch, out).wait_recv()
+
+            @pl.when(sends & has_in & mine)
+            def _():
+                for k in range(ch * per, ch * per + per):
+                    out[o, k] = (ready[way, k] + got[o, k].astype(F32)).astype(BF16)
+                copy(o, ch, out).start()
+
+            @pl.when(sends & has_in & jnp.logical_not(mine))
+            def _():
+                copy(o, ch, got).start()
+
+            @pl.when(sends & jnp.logical_not(has_in) & mine)
+            def _():
+                for k in range(ch * per, ch * per + per):
+                    out[o, k] = ready[way, k].astype(BF16)
+                copy(o, ch, out).start()
+
+            @pl.when(sends & jnp.logical_not(has_in) & jnp.logical_not(mine))
+            def _():
+                far_copy(way, o, ch).start()
+
+    def step(s, carry):
+        for ch in range(cut):
+            fwd_step(s, ch)
+            bwd_step(s - lag, ch)
+        deliver(s)
+
+        @pl.when(s == 1)
         def _():
-            for d in range(1, ny):
-                y_back(d).wait_recv()
-
-        @pl.when(s >= LAG)
-        def _():
-            bwd_step(s - LAG)
-
-        @pl.when(s == 3)
-        def _():
-            blocks_far.wait_recv()
-            forward_col(1, far)
-
+            forward_col(0, g)
+
+        prepare(s + 1 - lag)
         if with_sum:
             for k in range(1, len(ar)):
                 @pl.when(s == k)
@@ -317,63 +370,56 @@
                     ar[k]()
         return carry
 
-    lax.fori_loop(1, max(nz + LAG - 1, 10), step, 0)
-
+    if lag == 1:
+        prepare(0)
+    lax.fori_loop(1, max(nz + lag, 10), step, 0)
+
+    y_arrived(z)
     for k in range(own_count):
         back[k] = placed(z, k) + placed_col(zh, 0, k)
-
-    @pl.when(z > 0)
-    def _():
-        back_right(z).wait_recv()
-        for k in range(own_count):
-            back[k] += from_left[z, k].astype(F32)
-
-    @pl.when(z < nz - 1)
-    def _():
-        back_left(z).wait_recv()
-        for k in range(own_count):
-            back[k] += from_right[z, k].astype(F32)
-
-    back_far.wait_recv()
-    for k in range(own_count):
-        back[k] += far_in[k].astype(F32)
+    for way, copy, got, some in (
+        (0, back_left, in_right, reach_right(z) > 0), (1, back_right, in_left, reach_left(z) > 0)
+    ):
+        @pl.when(some)
+        def _():
+            for ch in range(cut):
+                copy(g, ch, got).wait_recv()
+            for k in range(own_count):
+                back[k] += got[g, k].astype(F32)
 
     def arrive(src, carry):
         for d in range(1, ny):
             y_in(d, src).wait_recv()
             y_out(d, src).wait_send()
-
-        @pl.when((src <= z) & (z < nz - 1))
-        def _():
-            right(src).wait_send()
-
-        @pl.when((src >= z) & (z > 0))
-        def _():
-            left(src).wait_send()
-
-        @pl.when(src > z)
-        def _():
-            back_right(src).wait_send()
-
-        @pl.when(src < z)
-        def _():
-            back_left(src).wait_send()
-
+            y_back(d, src).wait_send()
         return carry
 
     lax.fori_loop(0, nz, arrive, 0)
+
+    def sent(s, carry):
+        for way, copy, back_copy, buf in ((0, right, back_left, out_left), (1, left, back_right, out_right)):
+            src, low, comes, goes_on, mine = coming(s, way)
+
+            @pl.when((comes | (s == 0)) & goes_on)
+            def _():
+                for ch in range(cut):
+                    copy(src, ch).wait_send()
+
+            @pl.when(comes)
+            def _():
+                for ch in range(cut):
+                    back_copy(src, ch, buf).wait_send()
+        return carry
+
+    lax.fori_loop(0, nz + 1, sent, 0)
     for d in range(1, nx):
         for s in range(2):
             c_in(d, s).wait_recv()
             c_out(d, s).wait_send()
         x_back(d).wait_send()
-    for d in range(1, ny):
-        y_back(d).wait_send()
     for d in range(1, nz):
         idx_copy(d).wait_send()
     idx_far.wait_send()
-    blocks_far.wait_send()
-    back_far.wait_send()
 
 
 def sum_stages(split, gr, gout, refs, where, remote):
@@ -513,9 +559,10 @@
     blocks = (own_count, rows, feat)
     one = (rows, feat)
     dma = pltpu.SemaphoreType.DMA
+    ring = nh * nz
+    pieces = dma((ring, CUT))
     scratch = [
-        pltpu.VMEM((nz,) + blocks, BF16),
-        pltpu.VMEM(blocks, BF16),
+        pltpu.VMEM((ring,) + blocks, BF16),
         pltpu.VMEM((nz + 1, 8, 128), jnp.int32),
         pltpu.VMEM((ny, nz, 8, 128), F32),
         pltpu.VMEM((nx, 2, 8, 128), F32),
@@ -523,16 +570,16 @@
         pltpu.VMEM((nx, 2) + one, BF16),
         pltpu.VMEM((ny, nz) + one, BF16),
         pltpu.VMEM((nx, nh) + one, BF16),
-        pltpu.VMEM((nz,) + blocks, BF16),
-        pltpu.VMEM((nz,) + blocks, BF16),
-        pltpu.VMEM((nz,) + blocks, BF16),
-        pltpu.VMEM((nz,) + blocks, BF16),
-        pltpu.VMEM(blocks, BF16),
-        pltpu.VMEM(blocks, BF16),
-        dma((nz,)), dma((nz + 1,)), dma((nz,)), dma((nz,)), dma((nz,)), dma((2,)), dma((2,)),
+        pltpu.VMEM((ring,) + blocks, BF16),
+        pltpu.VMEM((ring,) + blocks, BF16),
+        pltpu.VMEM((ring,) + blocks, BF16),
+        pltpu.VMEM((ring,) + blocks, BF16),
+        pltpu.VMEM((2,) + blocks, F32),
+        pltpu.VMEM((1,) + blocks, BF16),
+        dma((nz,)), dma((nz + 1,)), pieces, pieces, pieces,
         dma((ny, nz)), dma((ny, nz)), dma((nx, 2)), dma((nx, 2)),
-        dma((ny,)), dma((ny,)), dma((nx,)), dma((nx,)),
-        dma((nz,)), dma((nz,)), dma((nz,)), dma((nz,)),
+        dma((ny, nz)), dma((ny, nz)), dma((nx,)), dma((nx,)),
+        pieces, pieces, pieces, pieces,
     ]
     out_shape = [
         jax.ShapeDtypeStruct((size, rows, feat), BF16),
@@ -563,7 +610,7 @@
         ]
     vmem = pl.BlockSpec(memory_space=pltpu.VMEM)
     return pl.pallas_call(
-        functools.partial(exchange_kernel, split, grads is not None),
+        functools.partial(exchange_kernel, split, LAG, CUT, grads is not None),
         out_shape=out_shape,
         in_specs=[vmem] * len(args),
         out_specs=[vmem] * len(out_shape),

time: 184 us -> 154 us (0.84)
  the two profiles are of different devices: /device:TPU:32 before, /device:TPU:64 now
where the time goes in v2:
time: 154 us; the launch traced here: 153 us
  Pallas kernels  147 us (95%)
  local copies, waits for them, and re-layouts  5.02 us (3%)
    pallas_call x2, Pallas kernels, exchange(): pl.pallas_call(functools.partial(exchange_kernel, split, LAG, CUT, grads...  134 us
    pallas_call x3, Pallas kernels, on_device(): pl.pallas_call(body, out_shape=out_shape, in_specs=[smem] * len(edges) +...  12.3 us
    unnamed x20, local copies, waits for them, and re-layouts  4.31 us

profile of v2, /device:TPU:64, one launch (start us, length us, event | category | flops | bytes accessed | tf_op | source)
XLA Modules:
  0.0 153.3 jit_solution(12162618151913139410)
XLA Ops:
  0.6 0.7 pad_add_fusion
  1.4 0.0 copy-start
  1.4 1.2 copy-done
  2.6 0.0 copy-start.2
  2.6 0.9 copy-done.2
  3.5 0.0 copy-start.8
  3.5 0.7 copy-done.8
  4.1 0.0 copy-start.9
  4.1 0.7 copy-done.9
  4.8 0.0 copy-start.1
  4.8 0.0 copy-start.4
  4.8 0.0 copy-start.5
  4.8 0.0 copy-start.6
  4.8 0.0 copy-start.7
  4.8 4.1 %shard_map.154 = (f32[4,128,128]{2,1,0:T(8,128)S(1)}, f32[4,128,128]{2,1,0:T(8,128)S(1)}, bf16[48,128,128]{2,1,0:T(8,128)(2,1)S(1)}) custom-call(s32[28]{0:T(128)S(1)} %bitcast.16, s32[28]{0:T(128)S(1)} %bitcast.19, bf16[28,128,128]{2,1,0:T(8,128)(2,1)S(1)} %bitcast.9, bf16[4,128,128]{2,1,0:T(8,128)(2,1)S(1)} %bitcast.12), custom_call_target="tpu_custom_call" | custom-call | tf_op jit(solution)/shard_map/pallas_call | solution.py:722
  8.9 0.0 copy-start.3
  8.9 0.9 copy-done.3
  9.8 68.0 %shard_map.155 = (bf16[52,128,128]{2,1,0:T(8,128)(2,1)S(1)}, f32[4,128,128]{2,1,0:T(8,128)S(1)}) custom-call(bf16[4,128,128]{2,1,0:T(8,128)(2,1)S(1)} %bitcast.14, bf16[48,128,128]{2,1,0:T(8,128)(2,1)S(1)} %get-tuple-element.20.refs_1_, s32[8,128]{1,0:T(8,128)S(1)} %broadcast_in_dim.2.refs_2_), custom_call_target="tpu_custom_call" | custom-call | tf_op jit(solution)/shard_map/pallas_call | solution.py:612
  77.8 0.0 copy-done.1
  77.8 0.0 copy-done.4
  77.8 0.0 copy-done.5
  77.8 0.0 copy-done.6
  77.8 0.0 copy-done.7
  77.8 5.5 %shard_map.156 = (bf16[4,128,128]{2,1,0:T(8,128)(2,1)S(1)}, f32[4,128,128]{2,1,0:T(8,128)S(1)}, bf16[48,128,128]{2,1,0:T(8,128)(2,1)S(1)}, f32[512,128]{1,0:T(8,128)S(1)}) custom-call(s32[28]{0:T(128)S(1)} %bitcast.17, s32[28]{0:T(128)S(1)} %bitcast.20, bf16[28,128,128]{2,1,0:T(8,128)(2,1)S(1)} %bitcast.10, bf16[4,128,128]{2,1,0:T(8,128)(2,1)S(1)} %bitcast.15, ...), custom_call_target="tpu_custom_call" | custom-call | tf_op jit(solution)/shard_map/pallas_call | solution.py:722
  83.3 66.5 %shard_map.157 = (bf16[52,128,128]{2,1,0:T(8,128)(2,1)S(1)}, f32[4,128,128]{2,1,0:T(8,128)S(1)}, f32[512,128]{1,0:T(8,128)S(1)}) custom-call(bf16[4,128,128]{2,1,0:T(8,128)(2,1)S(1)} %get-tuple-element.25.refs_0_.hidden, bf16[48,128,128]{2,1,0:T(8,128)(2,1)S(1)} %get-tuple-element.26.refs_1_, s32[8,128]{1,0:T(8,128)S(1)} %broadcast_in_dim.2.refs_2_, ...), custom_call_target="tpu_custom_call" | custom-call | tf_op jit(solution)/shard_map/pallas_call | solution.py:612
  149.8 2.7 %shard_map.158 = (bf16[4,128,128]{2,1,0:T(8,128)(2,1)}, f32[4,128,128]{2,1,0:T(8,128)}) custom-call(s32[28]{0:T(128)S(1)} %bitcast.18, s32[28]{0:T(128)S(1)} %bitcast.21, bf16[28,128,128]{2,1,0:T(8,128)(2,1)S(1)} %bitcast.11, bf16[4,128,128]{2,1,0:T(8,128)(2,1)S(1)} %get-tuple-element.25.refs_0_.hidden, bf16[52,128,128]{2,1,0:T(8,128)(2,1)S(1)} %get-tuple-element.28.table, ...), custom_call_target="tpu_custom_call" | custom-call | tf_op jit(solution)/shard_map/pallas_call | solution.py:722
  152.6 0.7 fusion
  (2 shorter events, 0.0 us)
Async XLA Ops:
  1.4 1.2 copy-start
  2.6 0.9 copy-start.2
  3.5 0.7 copy-start.8
  4.1 0.7 copy-start.9
  4.8 73.0 %copy-start.1 = (bf16[1,1,28,128,128]{4,3,2,1,0:T(8,128)(2,1)S(1)}, bf16[1,1,28,128,128]{4,3,2,1,0:T(8,128)(2,1)}, u32[]{:S(2)}) copy-start(bf16[1,1,28,128,128]{4,3,2,1,0:T(8,128)(2,1)} %param.12) | copy-start | bytes 2752516
  4.8 73.0 %copy-start.4 = (bf16[128,128]{1,0:T(8,128)(2,1)S(1)}, bf16[128,128]{1,0:T(8,128)(2,1)}, u32[]{:S(2)}) copy-start(bf16[128,128]{1,0:T(8,128)(2,1)} %ws2.3) | copy-start | bytes 98308
  4.8 73.0 %copy-start.5 = (bf16[128,128]{1,0:T(8,128)(2,1)S(1)}, bf16[128,128]{1,0:T(8,128)(2,1)}, u32[]{:S(2)}) copy-start(bf16[128,128]{1,0:T(8,128)(2,1)} %wn2.3) | copy-start | bytes 98308
  4.8 73.0 %copy-start.6 = (bf16[128,128]{1,0:T(8,128)(2,1)S(1)}, bf16[128,128]{1,0:T(8,128)(2,1)}, u32[]{:S(2)}) copy-start(bf16[128,128]{1,0:T(8,128)(2,1)} %ws1.1) | copy-start | bytes 98308
  4.8 73.0 %copy-start.7 = (bf16[128,128]{1,0:T(8,128)(2,1)S(1)}, bf16[128,128]{1,0:T(8,128)(2,1)}, u32[]{:S(2)}) copy-start(bf16[128,128]{1,0:T(8,128)(2,1)} %wn1.1) | copy-start | bytes 98308
  8.9 0.9 copy-start.3

commit v3 on v2

--- a/solution.py
+++ b/solution.py
@@ -11,10 +11,10 @@
 MESH = pl.DeviceIdType.MESH
 BF16 = jnp.bfloat16
 F32 = jnp.float32
-LIMIT = 44 * 1024 * 1024
+LIMIT = 52 * 1024 * 1024
 SPLIT = {"y": 4, "z": 8, "zh": 2, "xc": 8}
-LAG = 2
 CUT = 2
+UNIT = 16
 
 
 def dot(a, b):
@@ -29,77 +29,71 @@
     return lax.dot_general(a, b, (((0,), (0,)), ((), ())), preferred_element_type=F32)
 
 
-def exchange_kernel(split, lag, cut, with_sum, *refs):
-    ny, nz, nh, nx = split["y"], split["z"], split["zh"], split["xc"]
-    nrow, ring = ny * nz, nh * nz
-    refs = list(refs)
-    own, gsend, idx = refs[:3]
-    del refs[:3]
-    if with_sum:
-        gr = refs.pop(0)
-    table, back = refs[:2]
-    del refs[:2]
-    if with_sum:
-        gout = refs.pop(0)
-    (chain, tiles, pick_row, pick_col, stage_y, stage_c, land_y, land_c, in_right, in_left,
-     out_left, out_right, ready, far_out) = refs[:14]
-    (i_s, i_r, f_r, f_sr, f_sl, yf_s, yf_r, cf_s, cf_r, yb_s, yb_r, cb_s, cb_r,
-     br_r, bl_r, b_sl, b_sr) = refs[14:31]
-    own_count, rows, feat = own.shape
-    per = own_count // cut
-
-    r = lax.axis_index("row")
-    c = lax.axis_index("col")
-    y, z = lax.div(r, nz), lax.rem(r, nz)
-    zh, xc = lax.div(c, nx), lax.rem(c, nx)
-    g = zh * nz + z
-    partner = (1 - zh) * nx + xc
-
-    def y_peer(d):
-        return lax.rem(y + d, ny)
-
-    def x_peer(d):
-        return lax.rem(xc + d, nx)
-
-    def at_ring(pos):
-        pos = lax.rem(pos + ring, ring)
-        return y * nz + lax.rem(pos, nz), lax.div(pos, nz) * nx + xc
-
-    def reach_right(src):
-        return jnp.where(src < nz // 2, nz, nz - 1 - src)
-
-    def reach_left(src):
-        return jnp.where(src < nz // 2, src, nz)
-
-    def remote(src, dst, ssem, rsem, row, col):
-        return pltpu.make_async_remote_copy(
-            src_ref=src, dst_ref=dst, send_sem=ssem, recv_sem=rsem,
-            device_id=(row, col), device_id_type=MESH,
-        )
-
+class Place:
+    def __init__(self, split):
+        self.split = split
+        self.ny, self.nz, self.nh, self.nx = split["y"], split["z"], split["zh"], split["xc"]
+        self.nrow, self.ring = self.ny * self.nz, self.nh * self.nz
+        self.r = lax.axis_index("row")
+        self.c = lax.axis_index("col")
+        self.y, self.z = lax.div(self.r, self.nz), lax.rem(self.r, self.nz)
+        self.zh, self.xc = lax.div(self.c, self.nx), lax.rem(self.c, self.nx)
+        self.g = self.zh * self.nz + self.z
+        self.partner = (1 - self.zh) * self.nx + self.xc
+
+    def y_peer(self, d):
+        return lax.rem(self.y + d, self.ny)
+
+    def x_peer(self, d):
+        return lax.rem(self.xc + d, self.nx)
+
+    def at_ring(self, pos):
+        pos = lax.rem(pos + self.ring, self.ring)
+        return self.y * self.nz + lax.rem(pos, self.nz), lax.div(pos, self.nz) * self.nx + self.xc
+
+    def reach_right(self, src):
+        return jnp.where(src < self.nz // 2, self.nz, self.nz - 1 - src)
+
+    def reach_left(self, src):
+        return jnp.where(src < self.nz // 2, src, self.nz)
+
+
+def remote(src, dst, ssem, rsem, row, col):
+    return pltpu.make_async_remote_copy(
+        src_ref=src, dst_ref=dst, send_sem=ssem, recv_sem=rsem,
+        device_id=(row, col), device_id_type=MESH,
+    )
+
+
+def greet_all(place):
     barrier = pltpu.get_barrier_semaphore()
+    y, z, zh, g, r, c = place.y, place.z, place.zh, place.g, place.r, place.c
+    ny, nz, nx = place.ny, place.nz, place.nx
 
     def greet(row, col):
         pl.semaphore_signal(barrier, inc=1, device_id=(row, col), device_id_type=MESH)
 
-    for d in range(1, ny):
-        greet(y_peer(d) * nz + z, c)
+    greet(r, place.partner)
     for d in range(1, nz):
         greet(y * nz + lax.rem(z + d, nz), c)
-    greet(r, partner)
+    for d in range(1, ny):
+        greet(place.y_peer(d) * nz + z, c)
     for d in range(1, nx):
-        greet(r, zh * nx + x_peer(d))
-    at_end = (z == 0) | (z == nz - 1)
+        greet(r, zh * nx + place.x_peer(d))
 
     @pl.when(z == 0)
     def _():
-        greet(*at_ring(g - 1))
+        greet(*place.at_ring(g - 1))
 
     @pl.when(z == nz - 1)
     def _():
-        greet(*at_ring(g + 1))
-
-    met = (ny - 1) + (nz - 1) + 1 + (nx - 1)
+        greet(*place.at_ring(g + 1))
+
+
+def await_all(place):
+    barrier = pltpu.get_barrier_semaphore()
+    met = (place.ny - 1) + (place.nz - 1) + 1 + (place.nx - 1)
+    at_end = (place.z == 0) | (place.z == place.nz - 1)
 
     @pl.when(at_end)
     def _():
@@ -109,15 +103,20 @@
     def _():
         pl.semaphore_wait(barrier, met)
 
-    def idx_copy(d):
-        zz = lax.rem(z + d, nz)
-        return remote(idx, tiles.at[z], i_s.at[d], i_r.at[z], y * nz + zz, c)
-
-    def idx_wait(d):
-        zz = lax.rem(z + d, nz)
-        return remote(idx, tiles.at[zz], i_s.at[d], i_r.at[zz], y * nz + zz, c)
-
-    idx_far = remote(idx, tiles.at[nz], i_s.at[0], i_r.at[nz], r, partner)
+
+def phase(place, cut, own, table, back, picks, scratch, lists, fill, sums):
+    ny, nz, nh, nx = place.ny, place.nz, place.nh, place.nx
+    nrow, ring = place.nrow, place.ring
+    r, c, y, z, zh, xc, g = place.r, place.c, place.y, place.z, place.zh, place.xc, place.g
+    y_peer, x_peer, at_ring = place.y_peer, place.x_peer, place.at_ring
+    reach_right, reach_left = place.reach_right, place.reach_left
+    pick_row, pick_col = picks
+    (gsend, chain, stage_y, stage_c, land_y, land_c, in_right, in_left,
+     out_left, out_right, ready, far_out,
+     f_r, f_sr, f_sl, yf_s, yf_r, cf_s, cf_r, yb_s, yb_r, cb_s, cb_r,
+     br_r, bl_r, b_sl, b_sr) = scratch
+    own_count, rows, feat = own.shape
+    per = own_count // cut
 
     def part(ref, slot, ch):
         return ref.at[slot, pl.ds(ch * per, per)]
@@ -170,11 +169,7 @@
         return remote(stage_c.at[d, s], table.at[col_slot(s, xx)],
                       cf_s.at[d, s], cf_r.at[d, s], r, zh * nx + xx)
 
-    for d in range(1, nz):
-        idx_copy(d).start()
-    idx_far.start()
     chain[g] = own[...]
-    tiles[z] = idx[...]
     for ch in range(cut):
         @pl.when(reach_right(z) > 0)
         def _(ch=ch):
@@ -184,6 +179,7 @@
         def _(ch=ch):
             left(g, ch).start()
 
+    fill(gsend)
     for d in range(1, nx):
         x_back(d).start()
 
@@ -198,27 +194,12 @@
 
     lax.fori_loop(0, nz, first_y, 0)
 
-    if with_sum:
-        ar = sum_stages(split, gr, gout, refs[31:], (r, c, y, z, zh, xc), remote)
-        ar[0]()
+    if sums is not None:
+        sums[0]()
 
     table[pl.ds(0, own_count)] = own[...]
     land_y[0] = gsend[pl.ds(y * nz, nz)]
     land_c[0] = gsend[pl.ds(nrow + xc * nh, nh)]
-
-    for d in range(1, nz):
-        idx_wait(d).wait_recv()
-    idx_far.wait_recv()
-    lists = tiles[...].astype(F32)
-    along = lists[:nz].reshape(nz * 8, 128).astype(BF16)
-    pair = jnp.concatenate([tiles[z].astype(F32), lists[nz]], axis=0).astype(BF16)
-    lane = lax.broadcasted_iota(jnp.int32, (128, 128), 0)
-    for d in range(ny):
-        hot = jnp.where(lane == y_peer(d) * nz + z, 1.0, 0.0).astype(BF16)
-        pick_row[d] = dot(along, hot).reshape(nz, 8, 128)
-    for d in range(nx):
-        hot = jnp.where(lane == nrow + zh * nx + x_peer(d), 1.0, 0.0).astype(BF16)
-        pick_col[d] = dot(pair, hot).reshape(2, 8, 128)
 
     def hot_row(which, k):
         return jnp.where(which[0:1, :] == k, 1.0, 0.0)
@@ -267,8 +248,6 @@
         for d in range(1, ny):
             y_back(d, o).wait_recv()
 
-    forward(z)
-
     def coming(s, way):
         src = lax.rem(g + ring - s if way == 0 else g + s, ring)
         low = lax.rem(src, nz)
@@ -354,25 +333,28 @@
 
     def step(s, carry):
         for ch in range(cut):
-            fwd_step(s, ch)
-            bwd_step(s - lag, ch)
+            @pl.when(s > 1)
+            def _(ch=ch):
+                fwd_step(s, ch)
+
+            bwd_step(s - 1, ch)
+        prepare(s)
         deliver(s)
-
-        @pl.when(s == 1)
-        def _():
-            forward_col(0, g)
-
-        prepare(s + 1 - lag)
-        if with_sum:
-            for k in range(1, len(ar)):
+        if sums is not None:
+            for k in range(1, len(sums)):
                 @pl.when(s == k)
                 def _(k=k):
-                    ar[k]()
+                    sums[k]()
         return carry
 
-    if lag == 1:
-        prepare(0)
-    lax.fori_loop(1, max(nz + lag, 10), step, 0)
+    for ch in range(cut):
+        fwd_step(1, ch)
+    if lists is not None:
+        lists()
+    prepare(0)
+    forward(z)
+    forward_col(0, g)
+    lax.fori_loop(1, max(nz + 1, 9 if sums is None else 10), step, 0)
 
     y_arrived(z)
     for k in range(own_count):
@@ -417,22 +399,60 @@
             c_in(d, s).wait_recv()
             c_out(d, s).wait_send()
         x_back(d).wait_send()
-    for d in range(1, nz):
-        idx_copy(d).wait_send()
-    idx_far.wait_send()
-
-
-def sum_stages(split, gr, gout, refs, where, remote):
-    ny, nz, nx = split["y"], split["z"], split["xc"] // 2
-    r, c, y, z, zh, xc = where
+
+
+def list_exchange(place, idx, tiles, picks, i_s, i_r):
+    ny, nz, nx, nrow = place.ny, place.nz, place.nx, place.nrow
+    y, z, zh, r, c = place.y, place.z, place.zh, place.r, place.c
+    pick_row, pick_col = picks
+
+    def idx_copy(d):
+        zz = lax.rem(z + d, nz)
+        return remote(idx, tiles.at[z], i_s.at[d], i_r.at[z], y * nz + zz, c)
+
+    def idx_wait(d):
+        zz = lax.rem(z + d, nz)
+        return remote(idx, tiles.at[zz], i_s.at[d], i_r.at[zz], y * nz + zz, c)
+
+    idx_far = remote(idx, tiles.at[nz], i_s.at[0], i_r.at[nz], r, place.partner)
+
+    def send():
+        idx_far.start()
+        for d in range(1, nz):
+            idx_copy(d).start()
+        tiles[z] = idx[...]
+
+    def pick():
+        for d in range(1, nz):
+            idx_wait(d).wait_recv()
+        idx_far.wait_recv()
+        lists = tiles[...].astype(F32)
+        along = lists[:nz].reshape(nz * 8, 128).astype(BF16)
+        pair = jnp.concatenate([tiles[z].astype(F32), lists[nz]], axis=0).astype(BF16)
+        lane = lax.broadcasted_iota(jnp.int32, (128, 128), 0)
+        for d in range(ny):
+            hot = jnp.where(lane == place.y_peer(d) * nz + z, 1.0, 0.0).astype(BF16)
+            pick_row[d] = dot(along, hot).reshape(nz, 8, 128)
+        for d in range(nx):
+            hot = jnp.where(lane == nrow + zh * nx + place.x_peer(d), 1.0, 0.0).astype(BF16)
+            pick_col[d] = dot(pair, hot).reshape(2, 8, 128)
+        for d in range(1, nz):
+            idx_copy(d).wait_send()
+        idx_far.wait_send()
+
+    return send, pick
+
+
+def sum_stages(place, gr, gout, refs):
+    ny, nz, sx = place.ny, place.nz, place.nx
+    nx = sx // 2
+    r, c, y, z, zh, xc = place.r, place.c, place.y, place.z, place.zh, place.xc
     core, x = lax.rem(xc, 2), lax.div(xc, 2)
     (a1, v1, a2, v2, a3, a4, a5, v5, w1, w2, s1, r1, s2, r2, s3, r3, s4, r4, s5, r5,
      s6, r6, s7, r7, s8, r8) = refs
     half = gr.shape[0] // 2
     part = half // nx
     piece = part // ny
-    sx = split["xc"]
-    partner = (1 - zh) * sx + xc
     other = zh * sx + x * 2 + (1 - core)
 
     def xcol(d):
@@ -444,7 +464,7 @@
         return yy, yy * nz + z
 
     def rows_of(i, n):
-        return pl.ds(pl.multiple_of(i * n, n), n)
+        return pl.ds(i * n, n)
 
     c1 = remote(gr.at[rows_of(1 - core, half)], a1, s1.at[0], r1.at[0], r, other)
 
@@ -461,7 +481,7 @@
         to = z if slot is None else zz
         return remote(a4.at[z], a4.at[to], s4.at[d], r4.at[to], y * nz + zz, c)
 
-    c5 = remote(v5.at[0], a5, s5.at[0], r5.at[0], r, partner)
+    c5 = remote(v5.at[0], a5, s5.at[0], r5.at[0], r, place.partner)
 
     def c6(d, slot):
         yy, row = yrow(d)
@@ -552,73 +572,39 @@
     return [t0, t1, t2, t3, t4, t5, t6, t7, t8]
 
 
-def exchange(split, own, gsend, idx, grads, collective_id):
-    ny, nz, nh, nx = split["y"], split["z"], split["zh"], split["xc"]
-    own_count, rows, feat = own.shape
-    size = own_count + ny * nz + nh * nx
-    blocks = (own_count, rows, feat)
-    one = (rows, feat)
-    dma = pltpu.SemaphoreType.DMA
-    ring = nh * nz
-    pieces = dma((ring, CUT))
-    scratch = [
-        pltpu.VMEM((ring,) + blocks, BF16),
-        pltpu.VMEM((nz + 1, 8, 128), jnp.int32),
-        pltpu.VMEM((ny, nz, 8, 128), F32),
-        pltpu.VMEM((nx, 2, 8, 128), F32),
-        pltpu.VMEM((ny, nz) + one, BF16),
-        pltpu.VMEM((nx, 2) + one, BF16),
-        pltpu.VMEM((ny, nz) + one, BF16),
-        pltpu.VMEM((nx, nh) + one, BF16),
-        pltpu.VMEM((ring,) + blocks, BF16),
-        pltpu.VMEM((ring,) + blocks, BF16),
-        pltpu.VMEM((ring,) + blocks, BF16),
-        pltpu.VMEM((ring,) + blocks, BF16),
-        pltpu.VMEM((2,) + blocks, F32),
-        pltpu.VMEM((1,) + blocks, BF16),
-        dma((nz,)), dma((nz + 1,)), pieces, pieces, pieces,
-        dma((ny, nz)), dma((ny, nz)), dma((nx, 2)), dma((nx, 2)),
-        dma((ny, nz)), dma((ny, nz)), dma((nx,)), dma((nx,)),
-        pieces, pieces, pieces, pieces,
-    ]
-    out_shape = [
-        jax.ShapeDtypeStruct((size, rows, feat), BF16),
-        jax.ShapeDtypeStruct(blocks, F32),
-    ]
-    args = [own, gsend, idx]
-    if grads is not None:
-        args.append(grads)
-        out_shape.append(jax.ShapeDtypeStruct(grads.shape, F32))
-        half = grads.shape[0] // 2
-        cx = nx // 2
-        part = half // cx
-        piece = part // ny
-        scratch += [
-            pltpu.VMEM((half, 128), F32),
-            pltpu.VMEM((half, 128), F32),
-            pltpu.VMEM((cx, part, 128), F32),
-            pltpu.VMEM((part, 128), F32),
-            pltpu.VMEM((ny, piece, 128), F32),
-            pltpu.VMEM((nz, piece, 128), F32),
-            pltpu.VMEM((piece, 128), F32),
-            pltpu.VMEM((1, piece, 128), F32),
-            pltpu.VMEM((part, 128), F32),
-            pltpu.VMEM((half, 128), F32),
-            dma((1,)), dma((1,)), dma((cx,)), dma((cx,)), dma((ny,)), dma((ny,)),
-            dma((nz,)), dma((nz,)), dma((1,)), dma((1,)), dma((ny,)), dma((ny,)),
-            dma((cx,)), dma((cx,)), dma((1,)), dma((1,)),
-        ]
-    vmem = pl.BlockSpec(memory_space=pltpu.VMEM)
-    return pl.pallas_call(
-        functools.partial(exchange_kernel, split, LAG, CUT, grads is not None),
-        out_shape=out_shape,
-        in_specs=[vmem] * len(args),
-        out_specs=[vmem] * len(out_shape),
-        scratch_shapes=scratch,
-        compiler_params=pltpu.CompilerParams(
-            collective_id=collective_id, has_side_effects=True, vmem_limit_bytes=LIMIT
-        ),
-    )(*args)
+class Links:
+    def __init__(self, meta, edges, own_count):
+        self.meta, self.edges, self.own_count = meta, edges, own_count
+
+    def prev_dst(self, e):
+        return self.meta[e]
+
+    def prev_slot(self, e):
+        return self.meta[self.edges + e]
+
+    def last_dst(self, b):
+        return self.meta[2 * self.edges + b]
+
+    def last_slot(self, i):
+        return self.meta[2 * self.edges + self.own_count + i]
+
+
+def edge_links(split, own_count, size, dst, src):
+    edges = dst.size
+    slot = grad_slot(split, own_count, src)
+    e = jnp.arange(edges, dtype=jnp.int32)
+    early = e[None, :] < e[:, None]
+
+    def latest(match):
+        found = jnp.max(jnp.where(match, e[None, :], -1), axis=1)
+        return jnp.where(found < 0, edges, found)
+
+    return jnp.concatenate([
+        latest((dst[None, :] == dst[:, None]) & early),
+        latest((slot[None, :] == slot[:, None]) & early),
+        latest(dst[None, :] == jnp.arange(own_count, dtype=jnp.int32)[:, None]),
+        latest(slot[None, :] == jnp.arange(size, dtype=jnp.int32)[:, None]),
+    ])
 
 
 def grad_slot(split, own_count, t):
@@ -628,59 +614,60 @@
     return jnp.where(t < first, t, first + nh * lax.rem(q, nx) + lax.div(q, nx))
 
 
-def spread(split, own_count, adj, dst, src, q, grad):
-    @pl.loop(0, grad.shape[0])
-    def _(i):
-        grad[i] = jnp.zeros(grad.shape[1:], F32)
-
+def running(edges, run, term, prev):
     def one(e, carry):
-        grad[grad_slot(split, own_count, src[e])] += dot_at(adj[e], q[dst[e]])
+        run[e] = term(e) + run[prev(e)]
         return carry
 
-    lax.fori_loop(0, adj.shape[0], one, 0, unroll=4)
-
-
-def gather(adj, dst, src, table, acc):
-    def one(e, carry):
-        acc[dst[e]] += dot(adj[e], table[src[e]])
-        return carry
-
-    lax.fori_loop(0, adj.shape[0], one, 0, unroll=4)
-
-
-def send_out(own_count, grad, gsend):
+    lax.fori_loop(0, edges, one, 0, unroll=4)
+
+
+def spread(links, adj, dst, q, run):
+    running(links.edges, run, lambda e: dot_at(adj[e], q[dst[e]]), links.prev_slot)
+
+
+def gather(links, adj, src, table, run):
+    running(links.edges, run, lambda e: dot(adj[e], table[src[e]]), links.prev_dst)
+
+
+def send_out(links, own_count, run, gsend):
     @pl.loop(0, gsend.shape[0])
     def _(i):
-        gsend[i] = grad[own_count + i].astype(BF16)
-
-
-def first_kernel(split, dst, src, adj, cot, deg, u_own, gsend, grad, q):
-    own_count = cot.shape[0]
-    deg[...] = jnp.ones_like(deg)
-    ones = jnp.ones(adj.shape[1:], BF16)
-
-    def one(e, carry):
-        deg[dst[e]] += dot(adj[e], ones)
-        return carry
-
-    lax.fori_loop(0, adj.shape[0], one, 0, unroll=4)
+        gsend[i] = run[links.last_slot(own_count + i)].astype(BF16)
+
+
+def main_kernel(split, scale, n_phase, dst, src, meta, adj, feat, cot, idx, ws1, wn1, ws2, wn2,
+                hidden, table2, deg, base, back, gout, *scratch):
+    place = Place(split)
+    greet_all(place)
+    scratch = list(scratch)
+    table1, u_own, u_back, q, keep, grads, run_d, run_s, tiles, pick_row, pick_col, i_s, i_r = scratch[:13]
+    first, second, rest = scratch[13:13 + n_phase], scratch[13 + n_phase:13 + 2 * n_phase], scratch[13 + 2 * n_phase:]
+    picks = (pick_row, pick_col)
+    own_count, rows, width = feat.shape
+    edges = adj.shape[0]
+    links = Links(meta, edges, own_count)
+    run_d[edges] = jnp.zeros((rows, width), F32)
+    run_s[edges] = jnp.zeros((rows, width), F32)
+
+    ones = jnp.ones((rows, rows), BF16)
+    running(edges, run_d, lambda e: dot(adj[e], ones), links.prev_dst)
     for b in range(own_count):
+        deg[b] = 1.0 + run_d[links.last_dst(b)]
         q[b] = (cot[b].astype(F32) / deg[b]).astype(BF16)
-    spread(split, own_count, adj, dst, src, q, grad)
+    spread(links, adj, dst, q, run_s)
     for b in range(own_count):
-        u_own[b] = grad[b] + q[b].astype(F32)
-    send_out(own_count, grad, gsend)
-
-
-def middle_kernel(split, scale, dst, src, adj, feat, table, deg, u_own, u_back, cot,
-                  ws1, wn1, ws2, wn2, hidden, base, gsend, grads, acc, grad, q):
-    own_count, rows, width = feat.shape
+        u_own[b] = run_s[links.last_slot(b)] + q[b].astype(F32)
+    send_out(links, own_count, run_s, first[0])
+
+    await_all(place)
+    send, pick = list_exchange(place, idx, tiles, picks, i_s, i_r)
+    send()
+    phase(place, CUT, feat, table1, u_back, picks, first, pick, lambda gsend: None, None)
+
+    gather(links, adj, src, table1, run_d)
     for b in range(own_count):
-        acc[b] = feat[b].astype(F32)
-    gather(adj, dst, src, table, acc)
-    g1, g2, g3, g4 = 0.0, 0.0, 0.0, 0.0
-    for b in range(own_count):
-        mean = (acc[b] / deg[b]).astype(BF16)
+        mean = ((feat[b].astype(F32) + run_d[links.last_dst(b)]) / deg[b]).astype(BF16)
         pre = dot(feat[b], ws1[...]) + dot(mean, wn1[...])
         s = 1.0 / (1.0 + jnp.exp(-pre))
         hid = (pre * s).astype(BF16)
@@ -693,30 +680,99 @@
         qb = (dot_bt(dpre, wn1[...]) / deg[b]).astype(BF16)
         q[b] = qb
         base[b] = dot_bt(dpre, ws1[...]) + qb.astype(F32)
-        g1 = g1 + dot_at(feat[b], dpre)
-        g2 = g2 + dot_at(mean, dpre)
-        g3 = g3 + dot_at(hid, cot[b])
-        g4 = g4 + (dot_at(hid, hi) + dot_at(hid, lo))
-    for i, g in enumerate((g1, g2, g3, g4)):
-        grads[pl.ds(i * width, width), :] = g * scale
-    spread(split, own_count, adj, dst, src, q, grad)
+        keep[0, b] = dpre
+        keep[1, b] = mean
+        keep[2, b] = hi
+        keep[3, b] = lo
+    def weights(b, total):
+        dpre = keep[0, b]
+        return (
+            total[0] + dot_at(feat[b], dpre),
+            total[1] + dot_at(keep[1, b], dpre),
+            total[2] + dot_at(hidden[b], cot[b]),
+            total[3] + (dot_at(hidden[b], keep[2, b]) + dot_at(hidden[b], keep[3, b])),
+        )
+
+    zero = jnp.zeros((width, width), F32)
+    for i, part in enumerate(lax.fori_loop(0, own_count, weights, (zero,) * 4)):
+        grads[pl.ds(i * width // UNIT, width // UNIT)] = (part * scale).reshape(width // UNIT, UNIT, width)
+
+    def fill(gsend):
+        spread(links, adj, dst, q, run_s)
+        for b in range(own_count):
+            base[b] += run_s[links.last_slot(b)]
+        send_out(links, own_count, run_s, gsend)
+
+    phase(place, CUT, hidden, table2, back, picks, second, None, fill,
+          sum_stages(place, grads, gout, rest))
+
+
+def phase_scratch(split, own_count, rows, feat):
+    ny, nz, nh, nx = split["y"], split["z"], split["zh"], split["xc"]
+    ring = nh * nz
+    blocks = (own_count, rows, feat)
+    one = (rows, feat)
+    dma = pltpu.SemaphoreType.DMA
+    pieces = dma((ring, CUT))
+    return [
+        pltpu.VMEM((ny * nz + nh * nx,) + one, BF16),
+        pltpu.VMEM((ring,) + blocks, BF16),
+        pltpu.VMEM((ny, nz) + one, BF16),
+        pltpu.VMEM((nx, 2) + one, BF16),
+        pltpu.VMEM((ny, nz) + one, BF16),
+        pltpu.VMEM((nx, nh) + one, BF16),
+        pltpu.VMEM((ring,) + blocks, BF16),
+        pltpu.VMEM((ring,) + blocks, BF16),
+        pltpu.VMEM((ring,) + blocks, BF16),
+        pltpu.VMEM((ring,) + blocks, BF16),
+        pltpu.VMEM((2,) + blocks, F32),
+        pltpu.VMEM((1,) + blocks, BF16),
+        pieces, pieces, pieces,
+        dma((ny, nz)), dma((ny, nz)), dma((nx, 2)), dma((nx, 2)),
+        dma((ny, nz)), dma((ny, nz)), dma((nx,)), dma((nx,)),
+        pieces, pieces, pieces, pieces,
+    ]
+
+
+def sum_scratch(split, units):
+    ny, nz, cx = split["y"], split["z"], split["xc"] // 2
+    half = units // 2
+    part = half // cx
+    piece = part // ny
+    dma = pltpu.SemaphoreType.DMA
+    return [
+        pltpu.VMEM((half, UNIT, 128), F32),
+        pltpu.VMEM((half, UNIT, 128), F32),
+        pltpu.VMEM((cx, part, UNIT, 128), F32),
+        pltpu.VMEM((part, UNIT, 128), F32),
+        pltpu.VMEM((ny, piece, UNIT, 128), F32),
+        pltpu.VMEM((nz, piece, UNIT, 128), F32),
+        pltpu.VMEM((piece, UNIT, 128), F32),
+        pltpu.VMEM((1, piece, UNIT, 128), F32),
+        pltpu.VMEM((part, UNIT, 128), F32),
+        pltpu.VMEM((half, UNIT, 128), F32),
+        dma((1,)), dma((1,)), dma((cx,)), dma((cx,)), dma((ny,)), dma((ny,)),
+        dma((nz,)), dma((nz,)), dma((1,)), dma((1,)), dma((ny,)), dma((ny,)),
+        dma((cx,)), dma((cx,)), dma((1,)), dma((1,)),
+    ]
+
+
+def last_kernel(dst, src, meta, adj, hidden, table, deg, base, back, grads, ws2, wn2,
+                out, grad_in, g1, g2, g3, g4, run):
+    own_count, rows, width = hidden.shape
+    edges = adj.shape[0]
+    links = Links(meta, edges, own_count)
+    run[edges] = jnp.zeros((rows, width), F32)
+    gather(links, adj, src, table, run)
     for b in range(own_count):
-        base[b] += grad[b]
-    send_out(own_count, grad, gsend)
-
-
-def last_kernel(dst, src, adj, hidden, table, deg, base, back, ws2, wn2, out, grad_in, acc):
-    own_count = hidden.shape[0]
-    for b in range(own_count):
-        acc[b] = hidden[b].astype(F32)
-    gather(adj, dst, src, table, acc)
-    for b in range(own_count):
-        mean = (acc[b] / deg[b]).astype(BF16)
+        mean = ((hidden[b].astype(F32) + run[links.last_dst(b)]) / deg[b]).astype(BF16)
         out[b] = (dot(hidden[b], ws2[...]) + dot(mean, wn2[...])).astype(BF16)
         grad_in[b] = base[b] + back[b]
-
-
-def on_device(body, edges, args, out_shape, scratch):
+    for i, g in enumerate((g1, g2, g3, g4)):
+        g[...] = grads[pl.ds(i * width // UNIT, width // UNIT)].reshape(width, width)
+
+
+def call(body, edges, args, out_shape, scratch, params):
     smem = pl.BlockSpec(memory_space=pltpu.SMEM)
     vmem = pl.BlockSpec(memory_space=pltpu.VMEM)
     return pl.pallas_call(
@@ -725,7 +781,7 @@
         in_specs=[smem] * len(edges) + [vmem] * len(args),
         out_specs=[vmem] * len(out_shape),
         scratch_shapes=scratch,
-        compiler_params=pltpu.CompilerParams(vmem_limit_bytes=LIMIT),
+        compiler_params=pltpu.CompilerParams(vmem_limit_bytes=LIMIT, **params),
     )(*edges, *args)
 
 
@@ -746,49 +802,55 @@
 ):
     own = features[0, 0]
     adj = adjacency[0, 0]
-    edges = (edge_dst[0, 0], edge_src[0, 0])
+    dst, src = edge_dst[0, 0], edge_src[0, 0]
     cot = cotangent[0, 0]
     own_count, rows, width = own.shape
     lists = jnp.concatenate([send_row.reshape(-1), send_col.reshape(-1)])
     remote_count = lists.size
     idx = jnp.broadcast_to(jnp.pad(lists, (0, 128 - remote_count))[None, :], (8, 128))
     size = own_count + remote_count
+    edges = (dst, src, edge_links(split, own_count, size, dst, src))
     blocks = (own_count, rows, width)
     full = jax.ShapeDtypeStruct(blocks, F32)
     half = jax.ShapeDtypeStruct(blocks, BF16)
-    sends = jax.ShapeDtypeStruct((remote_count, rows, width), BF16)
-    grad = pltpu.VMEM((size, rows, width), F32)
-    acc = pltpu.VMEM(blocks, F32)
-    q = pltpu.VMEM(blocks, BF16)
-    deg, u_own, gsend = on_device(
-        functools.partial(first_kernel, split), edges, (adj, cot), [full, full, sends], [grad, q]
+    weight = jax.ShapeDtypeStruct((width, width), F32)
+    run = pltpu.VMEM((adj.shape[0] + 1, rows, width), F32)
+    ny, nz, nx = split["y"], split["z"], split["xc"]
+    dma = pltpu.SemaphoreType.DMA
+    per_phase = phase_scratch(split, own_count, rows, width)
+    scratch = [
+        pltpu.VMEM((size, rows, width), BF16),
+        pltpu.VMEM(blocks, F32),
+        pltpu.VMEM(blocks, F32),
+        pltpu.VMEM(blocks, BF16),
+        pltpu.VMEM((4,) + blocks, BF16),
+        pltpu.VMEM((4 * width // UNIT, UNIT, width), F32),
+        run,
+        run,
+        pltpu.VMEM((nz + 1, 8, 128), jnp.int32),
+        pltpu.VMEM((ny, nz, 8, 128), F32),
+        pltpu.VMEM((nx, 2, 8, 128), F32),
+        dma((nz,)),
+        dma((nz + 1,)),
+    ] + per_phase + per_phase + sum_scratch(split, 4 * width // UNIT)
+    hidden, table, deg, base, back, grads = call(
+        functools.partial(main_kernel, split, 1.0 / math.sqrt(nodes), len(per_phase)),
+        edges,
+        (adj, own, cot, idx, w_self1, w_neigh1, w_self2, w_neigh2),
+        [half, jax.ShapeDtypeStruct((size, rows, width), BF16), full, full, full,
+         jax.ShapeDtypeStruct((4 * width // UNIT, UNIT, width), F32)],
+        scratch,
+        dict(collective_id=0, has_side_effects=True),
     )
-    table, u_back = exchange(split, own, gsend, idx, None, 0)
-    weights = jax.ShapeDtypeStruct((4 * width, width), F32)
-    hidden, base, gsend, grads = on_device(
-        functools.partial(middle_kernel, split, 1.0 / math.sqrt(nodes)),
-        edges,
-        (adj, own, table, deg, u_own, u_back, cot, w_self1, w_neigh1, w_self2, w_neigh2),
-        [half, full, sends, weights],
-        [acc, grad, q],
-    )
-    table, back, grads = exchange(split, hidden, gsend, idx, grads, 1)
-    out, grad_in = on_device(
+    out, grad_in, g1, g2, g3, g4 = call(
         last_kernel,
         edges,
-        (adj, hidden, table, deg, base, back, w_self2, w_neigh2),
-        [half, full],
-        [acc],
+        (adj, hidden, table, deg, base, back, grads, w_self2, w_neigh2),
+        [half, full, weight, weight, weight, weight],
+        [run],
+        {},
     )
-    g = grads.reshape(4, width, width)
-    return (
-        out.reshape(features.shape),
-        grad_in.reshape(features.shape),
-        g[0],
-        g[1],
-        g[2],
-        g[3],
-    )
+    return out.reshape(features.shape), grad_in.reshape(features.shape), g1, g2, g3, g4
 
 
 def solution(mesh):

time: 154 us -> 147 us (0.955)
  the two profiles are of different devices: /device:TPU:64 before, /device:TPU:1 now
where the time goes in v3:
time: 147 us; the launch traced here: 145 us
  Pallas kernels  135 us (92%)
  local copies, waits for them, and re-layouts  6.16 us (4%)
  other arithmetic  3.47 us (2%)
    pallas_call x2, Pallas kernels, call(): pl.pallas_call(body, out_shape=out_shape, in_specs=[smem] * len(edges) +...  135 us
    unnamed x16, local copies, waits for them, and re-layouts  6.15 us

profile of v3, /device:TPU:1, one launch (start us, length us, event | category | flops | bytes accessed | tf_op | source)
XLA Modules:
  0.0 144.8 jit_solution(18126418348482952571)
XLA Ops:
  0.6 0.7 compare_select_fusion.3
  1.3 0.1 select_reduce_fusion
  1.4 0.2 select_reduce_fusion.1
  1.6 0.8 select_reduce_fusion.3
  2.4 0.9 select_reduce_fusion.2
  3.3 0.1 pad_add_fusion.meta
  3.4 0.7 pad_add_fusion.1
  4.1 0.0 copy-start
  4.1 0.8 copy-done
  4.9 0.0 copy-start.1
  4.9 0.8 copy-done.1
  5.6 0.0 copy-start.2
  5.6 0.9 copy-done.2
  6.6 0.0 copy-start.3
  6.6 0.9 copy-done.3
  7.5 0.0 copy-start.4
  7.5 0.8 copy-done.4
  8.2 0.0 copy-start.5
  8.2 0.8 copy-done.5
  9.0 0.0 copy-start.6
  9.0 0.7 copy-done.6
  9.6 0.0 copy-start.7
  9.6 0.7 copy-done.7
  10.3 130.5 %shard_map.154 = (bf16[4,128,128]{2,1,0:T(8,128)(2,1)S(1)}, bf16[52,128,128]{2,1,0:T(8,128)(2,1)}, f32[4,128,128]{2,1,0:T(8,128)S(1)}, f32[4,128,128]{2,1,0:T(8,...) custom-call(s32[28]{0:T(128)S(1)} %bitcast.14, s32[28]{0:T(128)S(1)} %bitcast.16, ...), custom_call_target="tpu_custom_call" | custom-call | tf_op jit(solution)/shard_map/pallas_call | solution.py:778
  140.8 4.0 %shard_map.155 = (bf16[4,128,128]{2,1,0:T(8,128)(2,1)}, f32[4,128,128]{2,1,0:T(8,128)}, f32[128,128]{1,0:T(8,128)}, f32[128,128]{1,0:T(8,128)}, f32[128,128]{1,0:T(8,128)}, /*index=5*/f32[128,128]{1,0:T(8,128)}) custom-call(s32[28]{0:T(128)S(1)} %bitcast.15, s32[28]{0:T(128)S(1)} %bitcast.17, s32[112]{0:T(128)S(1)} %pad_add_fusion.meta, ...), custom_call_target="tpu_custom_call" | custom-call | tf_op jit(solution)/shard_map/pallas_call | solution.py:778
  (5 shorter events, 0.0 us)
Async XLA Ops:
  4.1 0.8 copy-start
  4.9 0.8 copy-start.1
  5.6 0.9 copy-start.2
  6.6 0.9 copy-start.3
  7.5 0.8 copy-start.4
  8.2 0.8 copy-start.5
  9.0 0.7 copy-start.6
  9.6 0.7 copy-start.7

commit v4 on v3

--- a/solution.py
+++ b/solution.py
@@ -104,7 +104,7 @@
         pl.semaphore_wait(barrier, met)
 
 
-def phase(place, cut, own, table, back, picks, scratch, lists, fill, sums):
+def phase(place, cut, own, table, back, picks, scratch, lists, fill, after, sums):
     ny, nz, nh, nx = place.ny, place.nz, place.nh, place.nx
     nrow, ring = place.nrow, place.ring
     r, c, y, z, zh, xc, g = place.r, place.c, place.y, place.z, place.zh, place.xc, place.g
@@ -194,13 +194,6 @@
 
     lax.fori_loop(0, nz, first_y, 0)
 
-    if sums is not None:
-        sums[0]()
-
-    table[pl.ds(0, own_count)] = own[...]
-    land_y[0] = gsend[pl.ds(y * nz, nz)]
-    land_c[0] = gsend[pl.ds(nrow + xc * nh, nh)]
-
     def hot_row(which, k):
         return jnp.where(which[0:1, :] == k, 1.0, 0.0)
 
@@ -349,6 +342,12 @@
 
     for ch in range(cut):
         fwd_step(1, ch)
+    after()
+    if sums is not None:
+        sums[0]()
+    table[pl.ds(0, own_count)] = own[...]
+    land_y[0] = gsend[pl.ds(y * nz, nz)]
+    land_c[0] = gsend[pl.ds(nrow + xc * nh, nh)]
     if lists is not None:
         lists()
     prepare(0)
@@ -636,54 +635,69 @@
         gsend[i] = run[links.last_slot(own_count + i)].astype(BF16)
 
 
-def main_kernel(split, scale, n_phase, dst, src, meta, adj, feat, cot, idx, ws1, wn1, ws2, wn2,
-                hidden, table2, deg, base, back, gout, *scratch):
+def main_kernel(split, scale, n_phase, n_in, dst, src, meta, idx, *refs):
     place = Place(split)
     greet_all(place)
-    scratch = list(scratch)
-    table1, u_own, u_back, q, keep, grads, run_d, run_s, tiles, pick_row, pick_col, i_s, i_r = scratch[:13]
-    first, second, rest = scratch[13:13 + n_phase], scratch[13 + n_phase:13 + 2 * n_phase], scratch[13 + 2 * n_phase:]
+    far_in, refs = refs[:n_in], refs[n_in:]
+    (hidden, table2, deg, base, back, gout), refs = refs[:6], refs[6:]
+    near_in, refs = refs[:n_in], list(refs[n_in:])
+    (in_s, table1, u_own, u_back, q, keep, grads, run_d, run_s, tiles, pick_row, pick_col,
+     i_s, i_r) = refs[:14]
+    del refs[:14]
+    first, second, rest = refs[:n_phase], refs[n_phase:2 * n_phase], refs[2 * n_phase:]
+    feat, adj, cot, ws1, wn1, ws2, wn2 = near_in
+    loads = [pltpu.make_async_copy(a, b, in_s.at[i]) for i, (a, b) in enumerate(zip(far_in, near_in))]
+    for load in loads:
+        load.start()
     picks = (pick_row, pick_col)
     own_count, rows, width = feat.shape
     edges = adj.shape[0]
     links = Links(meta, edges, own_count)
     run_d[edges] = jnp.zeros((rows, width), F32)
     run_s[edges] = jnp.zeros((rows, width), F32)
-
-    ones = jnp.ones((rows, rows), BF16)
-    running(edges, run_d, lambda e: dot(adj[e], ones), links.prev_dst)
-    for b in range(own_count):
-        deg[b] = 1.0 + run_d[links.last_dst(b)]
-        q[b] = (cot[b].astype(F32) / deg[b]).astype(BF16)
-    spread(links, adj, dst, q, run_s)
-    for b in range(own_count):
-        u_own[b] = run_s[links.last_slot(b)] + q[b].astype(F32)
-    send_out(links, own_count, run_s, first[0])
-
+    loads[0].wait()
     await_all(place)
     send, pick = list_exchange(place, idx, tiles, picks, i_s, i_r)
     send()
-    phase(place, CUT, feat, table1, u_back, picks, first, pick, lambda gsend: None, None)
+
+    def fill_two(gsend):
+        for load in loads[1:]:
+            load.wait()
+        ones = jnp.ones((rows, rows), BF16)
+        running(edges, run_d, lambda e: dot(adj[e], ones), links.prev_dst)
+        for b in range(own_count):
+            deg[b] = 1.0 + run_d[links.last_dst(b)]
+            q[b] = (cot[b].astype(F32) / deg[b]).astype(BF16)
+        spread(links, adj, dst, q, run_s)
+        send_out(links, own_count, run_s, gsend)
+
+    def after_two():
+        for b in range(own_count):
+            u_own[b] = run_s[links.last_slot(b)] + q[b].astype(F32)
+
+    phase(place, CUT, feat, table1, u_back, picks, first, pick, fill_two, after_two, None)
 
     gather(links, adj, src, table1, run_d)
     for b in range(own_count):
         mean = ((feat[b].astype(F32) + run_d[links.last_dst(b)]) / deg[b]).astype(BF16)
         pre = dot(feat[b], ws1[...]) + dot(mean, wn1[...])
         s = 1.0 / (1.0 + jnp.exp(-pre))
-        hid = (pre * s).astype(BF16)
-        hidden[b] = hid
+        hidden[b] = (pre * s).astype(BF16)
         u = u_own[b] + u_back[b]
         hi = u.astype(BF16)
         lo = (u - hi.astype(F32)).astype(BF16)
         dh = dot_bt(cot[b], ws2[...]) + (dot_bt(hi, wn2[...]) + dot_bt(lo, wn2[...]))
         dpre = (dh * (s * (1.0 + pre * (1.0 - s)))).astype(BF16)
-        qb = (dot_bt(dpre, wn1[...]) / deg[b]).astype(BF16)
-        q[b] = qb
-        base[b] = dot_bt(dpre, ws1[...]) + qb.astype(F32)
+        q[b] = (dot_bt(dpre, wn1[...]) / deg[b]).astype(BF16)
         keep[0, b] = dpre
         keep[1, b] = mean
         keep[2, b] = hi
         keep[3, b] = lo
+
+    def fill_one(gsend):
+        spread(links, adj, dst, q, run_s)
+        send_out(links, own_count, run_s, gsend)
+
     def weights(b, total):
         dpre = keep[0, b]
         return (
@@ -693,17 +707,14 @@
             total[3] + (dot_at(hidden[b], keep[2, b]) + dot_at(hidden[b], keep[3, b])),
         )
 
-    zero = jnp.zeros((width, width), F32)
-    for i, part in enumerate(lax.fori_loop(0, own_count, weights, (zero,) * 4)):
-        grads[pl.ds(i * width // UNIT, width // UNIT)] = (part * scale).reshape(width // UNIT, UNIT, width)
-
-    def fill(gsend):
-        spread(links, adj, dst, q, run_s)
+    def after_one():
+        zero = jnp.zeros((width, width), F32)
+        for i, part in enumerate(lax.fori_loop(0, own_count, weights, (zero,) * 4)):
+            grads[pl.ds(i * width // UNIT, width // UNIT)] = (part * scale).reshape(width // UNIT, UNIT, width)
         for b in range(own_count):
-            base[b] += run_s[links.last_slot(b)]
-        send_out(links, own_count, run_s, gsend)
-
-    phase(place, CUT, hidden, table2, back, picks, second, None, fill,
+            base[b] = dot_bt(keep[0, b], ws1[...]) + q[b].astype(F32) + run_s[links.last_slot(b)]
+
+    phase(place, CUT, hidden, table2, back, picks, second, None, fill_one, after_one,
           sum_stages(place, grads, gout, rest))
 
 
@@ -772,17 +783,18 @@
         g[...] = grads[pl.ds(i * width // UNIT, width // UNIT)].reshape(width, width)
 
 
-def call(body, edges, args, out_shape, scratch, params):
+def call(body, edges, args, far, out_shape, scratch, params):
     smem = pl.BlockSpec(memory_space=pltpu.SMEM)
     vmem = pl.BlockSpec(memory_space=pltpu.VMEM)
+    where = pl.BlockSpec(memory_space=pl.ANY)
     return pl.pallas_call(
         body,
         out_shape=out_shape,
-        in_specs=[smem] * len(edges) + [vmem] * len(args),
+        in_specs=[smem] * len(edges) + [vmem] * len(args) + [where] * len(far),
         out_specs=[vmem] * len(out_shape),
         scratch_shapes=scratch,
         compiler_params=pltpu.CompilerParams(vmem_limit_bytes=LIMIT, **params),
-    )(*edges, *args)
+    )(*edges, *args, *far)
 
 
 def local(
@@ -818,7 +830,9 @@
     ny, nz, nx = split["y"], split["z"], split["xc"]
     dma = pltpu.SemaphoreType.DMA
     per_phase = phase_scratch(split, own_count, rows, width)
-    scratch = [
+    far = (own, adj, cot, w_self1, w_neigh1, w_self2, w_neigh2)
+    scratch = [pltpu.VMEM(a.shape, BF16) for a in far] + [
+        dma((len(far),)),
         pltpu.VMEM((size, rows, width), BF16),
         pltpu.VMEM(blocks, F32),
         pltpu.VMEM(blocks, F32),
@@ -834,9 +848,10 @@
         dma((nz + 1,)),
     ] + per_phase + per_phase + sum_scratch(split, 4 * width // UNIT)
     hidden, table, deg, base, back, grads = call(
-        functools.partial(main_kernel, split, 1.0 / math.sqrt(nodes), len(per_phase)),
+        functools.partial(main_kernel, split, 1.0 / math.sqrt(nodes), len(per_phase), len(far)),
         edges,
-        (adj, own, cot, idx, w_self1, w_neigh1, w_self2, w_neigh2),
+        (idx,),
+        far,
         [half, jax.ShapeDtypeStruct((size, rows, width), BF16), full, full, full,
          jax.ShapeDtypeStruct((4 * width // UNIT, UNIT, width), F32)],
         scratch,
@@ -846,6 +861,7 @@
         last_kernel,
         edges,
         (adj, hidden, table, deg, base, back, grads, w_self2, w_neigh2),
+        (),
         [half, full, weight, weight, weight, weight],
         [run],
         {},

time: 147 us -> 149 us (1.014)
  Pallas kernels: 135 us -> 137 us
    pallas_call x2, Pallas kernels: 135 us -> 137 us  [call(): pl.pallas_call(body, out_shape=out_shape, in_specs=[smem] * len(edges) +...]
where the time goes in v4:
time: 149 us; the launch traced here: 147 us
  Pallas kernels  137 us (92%)
  local copies, waits for them, and re-layouts  6.16 us (4%)
  other arithmetic  3.47 us (2%)
    pallas_call x2, Pallas kernels, call(): pl.pallas_call(body, out_shape=out_shape, in_specs=[smem] * len(edges) +...  137 us
    unnamed x16, local copies, waits for them, and re-layouts  6.15 us

profile of v4, /device:TPU:1, one launch (start us, length us, event | category | flops | bytes accessed | tf_op | source)
XLA Modules:
  0.0 146.8 jit_solution(5122333693610740380)
XLA Ops:
  0.6 0.7 compare_select_fusion.3
  1.3 0.1 select_reduce_fusion
  1.4 0.2 select_reduce_fusion.1
  1.6 0.8 select_reduce_fusion.3
  2.4 0.9 select_reduce_fusion.2
  3.3 0.1 pad_add_fusion.meta
  3.4 0.7 pad_add_fusion.1
  4.1 0.0 copy-start
  4.1 0.8 copy-done
  4.9 0.0 copy-start.1
  4.9 0.8 copy-done.1
  5.6 0.0 copy-start.2
  5.6 0.9 copy-done.2
  6.6 0.0 copy-start.3
  6.6 0.9 copy-done.3
  7.5 0.0 copy-start.4
  7.5 0.8 copy-done.4
  8.2 0.0 copy-start.5
  8.2 0.8 copy-done.5
  9.0 0.0 copy-start.6
  9.0 0.7 copy-done.6
  9.6 0.0 copy-start.7
  9.6 0.7 copy-done.7
  10.3 132.5 %shard_map.154 = (bf16[4,128,128]{2,1,0:T(8,128)(2,1)S(1)}, bf16[52,128,128]{2,1,0:T(8,128)(2,1)}, f32[4,128,128]{2,1,0:T(8,128)S(1)}, f32[4,128,128]{2,1,0:T(8,...) custom-call(s32[28]{0:T(128)S(1)} %bitcast.14, s32[28]{0:T(128)S(1)} %bitcast.16, ...), custom_call_target="tpu_custom_call" | custom-call | tf_op jit(solution)/shard_map/pallas_call | solution.py:790
  142.8 4.1 %shard_map.155 = (bf16[4,128,128]{2,1,0:T(8,128)(2,1)}, f32[4,128,128]{2,1,0:T(8,128)}, f32[128,128]{1,0:T(8,128)}, f32[128,128]{1,0:T(8,128)}, f32[128,128]{1,0:T(8,128)}, /*index=5*/f32[128,128]{1,0:T(8,128)}) custom-call(s32[28]{0:T(128)S(1)} %bitcast.15, s32[28]{0:T(128)S(1)} %bitcast.17, s32[112]{0:T(128)S(1)} %pad_add_fusion.meta, ...), custom_call_target="tpu_custom_call" | custom-call | tf_op jit(solution)/shard_map/pallas_call | solution.py:790
  (5 shorter events, 0.0 us)
Async XLA Ops:
  4.1 0.8 copy-start
  4.9 0.8 copy-start.1
  5.6 0.9 copy-start.2
  6.6 0.9 copy-start.3
  7.5 0.8 copy-start.4
  8.2 0.8 copy-start.5
  9.0 0.7 copy-start.6
  9.6 0.7 copy-start.7

commit v5 on v4

--- a/solution.py
+++ b/solution.py
@@ -11,7 +11,7 @@
 MESH = pl.DeviceIdType.MESH
 BF16 = jnp.bfloat16
 F32 = jnp.float32
-LIMIT = 52 * 1024 * 1024
+LIMIT = 60 * 1024 * 1024
 SPLIT = {"y": 4, "z": 8, "zh": 2, "xc": 8}
 CUT = 2
 UNIT = 16
@@ -324,6 +324,22 @@
             def _():
                 far_copy(way, o, ch).start()
 
+    def settle(s):
+        for way, copy in ((0, right), (1, left)):
+            src, low, comes, goes_on, mine = coming(s, way)
+
+            @pl.when((comes | (s == 0)) & goes_on)
+            def _():
+                for ch in range(cut):
+                    copy(src, ch).wait_send()
+
+            @pl.when((comes & mine) | ((s == 0) & (way == 0)))
+            def _():
+                for d in range(1, ny):
+                    y_in(d, low).wait_recv()
+                    y_out(d, low).wait_send()
+                    y_back(d, low).wait_send()
+
     def step(s, carry):
         for ch in range(cut):
             @pl.when(s > 1)
@@ -333,6 +349,36 @@
             bwd_step(s - 1, ch)
         prepare(s)
         deliver(s)
+
+        @pl.when(s == 1)
+        def _():
+            forward(z)
+
+        @pl.when(s == 3)
+        def _():
+            forward_col(0, g)
+
+        @pl.when(s == 5)
+        def _():
+            y_arrived(z)
+            for k in range(own_count):
+                back[k] = placed(z, k) + placed_col(zh, 0, k)
+
+        @pl.when(s == 6)
+        def _():
+            for d in range(1, nx):
+                x_back(d).wait_send()
+
+        @pl.when(s == 7)
+        def _():
+            for d in range(1, nx):
+                c_in(d, 0).wait_recv()
+                c_out(d, 0).wait_send()
+
+        @pl.when(s >= 3)
+        def _():
+            settle(s - 3)
+
         if sums is not None:
             for k in range(1, len(sums)):
                 @pl.when(s == k)
@@ -351,13 +397,9 @@
     if lists is not None:
         lists()
     prepare(0)
-    forward(z)
-    forward_col(0, g)
-    lax.fori_loop(1, max(nz + 1, 9 if sums is None else 10), step, 0)
-
-    y_arrived(z)
-    for k in range(own_count):
-        back[k] = placed(z, k) + placed_col(zh, 0, k)
+    last = max(nz + 1, 9 if sums is None else 10)
+    lax.fori_loop(1, last, step, 0)
+
     for way, copy, got, some in (
         (0, back_left, in_right, reach_right(z) > 0), (1, back_right, in_left, reach_left(z) > 0)
     ):
@@ -368,36 +410,22 @@
             for k in range(own_count):
                 back[k] += got[g, k].astype(F32)
 
-    def arrive(src, carry):
-        for d in range(1, ny):
-            y_in(d, src).wait_recv()
-            y_out(d, src).wait_send()
-            y_back(d, src).wait_send()
+    lax.fori_loop(last - 3, nz + 1, lambda s, carry: (settle(s), carry)[1], 0)
+
+    def sent(s, carry):
+        for way, copy, buf in ((0, back_left, out_left), (1, back_right, out_right)):
+            src, low, comes, goes_on, mine = coming(s, way)
+
+            @pl.when(comes)
+            def _():
+                for ch in range(cut):
+                    copy(src, ch, buf).wait_send()
         return carry
 
-    lax.fori_loop(0, nz, arrive, 0)
-
-    def sent(s, carry):
-        for way, copy, back_copy, buf in ((0, right, back_left, out_left), (1, left, back_right, out_right)):
-            src, low, comes, goes_on, mine = coming(s, way)
-
-            @pl.when((comes | (s == 0)) & goes_on)
-            def _():
-                for ch in range(cut):
-                    copy(src, ch).wait_send()
-
-            @pl.when(comes)
-            def _():
-                for ch in range(cut):
-                    back_copy(src, ch, buf).wait_send()
-        return carry
-
-    lax.fori_loop(0, nz + 1, sent, 0)
+    lax.fori_loop(1, nz + 1, sent, 0)
     for d in range(1, nx):
-        for s in range(2):
-            c_in(d, s).wait_recv()
-            c_out(d, s).wait_send()
-        x_back(d).wait_send()
+        c_in(d, 1).wait_recv()
+        c_out(d, 1).wait_send()
 
 
 def list_exchange(place, idx, tiles, picks, i_s, i_r):
@@ -655,27 +683,25 @@
     links = Links(meta, edges, own_count)
     run_d[edges] = jnp.zeros((rows, width), F32)
     run_s[edges] = jnp.zeros((rows, width), F32)
-    loads[0].wait()
+    for load in loads:
+        load.wait()
+
+    ones = jnp.ones((rows, rows), BF16)
+    running(edges, run_d, lambda e: dot(adj[e], ones), links.prev_dst)
+    for b in range(own_count):
+        deg[b] = 1.0 + run_d[links.last_dst(b)]
+        q[b] = (cot[b].astype(F32) / deg[b]).astype(BF16)
+    spread(links, adj, dst, q, run_s)
+    send_out(links, own_count, run_s, first[0])
     await_all(place)
     send, pick = list_exchange(place, idx, tiles, picks, i_s, i_r)
     send()
 
-    def fill_two(gsend):
-        for load in loads[1:]:
-            load.wait()
-        ones = jnp.ones((rows, rows), BF16)
-        running(edges, run_d, lambda e: dot(adj[e], ones), links.prev_dst)
-        for b in range(own_count):
-            deg[b] = 1.0 + run_d[links.last_dst(b)]
-            q[b] = (cot[b].astype(F32) / deg[b]).astype(BF16)
-        spread(links, adj, dst, q, run_s)
-        send_out(links, own_count, run_s, gsend)
-
     def after_two():
         for b in range(own_count):
             u_own[b] = run_s[links.last_slot(b)] + q[b].astype(F32)
 
-    phase(place, CUT, feat, table1, u_back, picks, first, pick, fill_two, after_two, None)
+    phase(place, CUT, feat, table1, u_back, picks, first, pick, lambda gsend: None, after_two, None)
 
     gather(links, adj, src, table1, run_d)
     for b in range(own_count):

time: 149 us -> 141 us (0.946)
  local copies, waits for them, and re-layouts: 6.16 us -> 0.6 us
  Pallas kernels: 137 us -> 133 us
    unnamed x16 -> x0, local copies, waits for them, and re-layouts: 6.15 us -> none
    pallas_call x2, Pallas kernels: 137 us -> 133 us  [call(): pl.pallas_call(body, out_shape=out_shape, in_specs=[smem] * len(edges) +...]
where the time goes in v5:
time: 141 us; the launch traced here: 139 us
  Pallas kernels  133 us (94%)
  other arithmetic  4.04 us (3%)
    pallas_call x2, Pallas kernels, call(): pl.pallas_call(body, out_shape=out_shape, in_specs=[smem] * len(edges) +...  133 us

profile of v5, /device:TPU:1, one launch (start us, length us, event | category | flops | bytes accessed | tf_op | source)
XLA Modules:
  0.0 138.5 jit_solution(9261651889653234453)
XLA Ops:
  0.6 0.7 compare_select_fusion.3
  1.3 0.1 select_reduce_fusion
  1.4 0.2 select_reduce_fusion.1
  1.6 0.8 select_reduce_fusion.3
  2.4 0.9 select_reduce_fusion.2
  3.3 0.7 pad_add_fusion.meta
  3.9 0.7 pad_add_fusion.1
  4.7 0.6 broadcast_in_dim.76.idx
  5.3 128.8 %shard_map.154 = (bf16[4,128,128]{2,1,0:T(8,128)(2,1)}, bf16[52,128,128]{2,1,0:T(8,128)(2,1)}, f32[4,128,128]{2,1,0:T(8,128)}, f32[4,128,128]{2,1,0:T(8,128)}, f...) custom-call(s32[28]{0:T(128)} %bitcast.16, s32[28]{0:T(128)} %bitcast.18, s32[112]{0:T(128)} %pad_add_fusion.meta, ...), custom_call_target="tpu_custom_call" | custom-call | tf_op jit(solution)/shard_map/pallas_call | solution.py:816
  134.1 4.4 %shard_map.155 = (bf16[4,128,128]{2,1,0:T(8,128)(2,1)}, f32[4,128,128]{2,1,0:T(8,128)}, f32[128,128]{1,0:T(8,128)}, f32[128,128]{1,0:T(8,128)}, f32[128,128]{1,0:T(8,128)}, /*index=5*/f32[128,128]{1,0:T(8,128)}) custom-call(s32[28]{0:T(128)} %bitcast.17, s32[28]{0:T(128)} %bitcast.19, s32[112]{0:T(128)} %pad_add_fusion.meta, bf16[28,128,128]{2,1,0:T(8,128)(2,1)} %bitcast.11, ...), custom_call_target="tpu_custom_call" | custom-call | tf_op jit(solution)/shard_map/pallas_call | solution.py:816
  (4 shorter events, 0.0 us)

commit v6 on v5

--- a/solution.py
+++ b/solution.py
@@ -3,6 +3,7 @@
 
 import jax
 import jax.numpy as jnp
+import numpy as np
 from jax import lax
 from jax.experimental import pallas as pl
 from jax.experimental.pallas import tpu as pltpu
@@ -179,9 +180,12 @@
         def _(ch=ch):
             left(g, ch).start()
 
-    fill(gsend)
+    if fill is not None:
+        fill[0](gsend)
     for d in range(1, nx):
         x_back(d).start()
+    if fill is not None:
+        fill[1](gsend)
 
     def first_y(i, carry):
         away = nz - 1 - i
@@ -619,19 +623,17 @@
 def edge_links(split, own_count, size, dst, src):
     edges = dst.size
     slot = grad_slot(split, own_count, src)
-    e = jnp.arange(edges, dtype=jnp.int32)
-    early = e[None, :] < e[:, None]
-
-    def latest(match):
-        found = jnp.max(jnp.where(match, e[None, :], -1), axis=1)
-        return jnp.where(found < 0, edges, found)
-
-    return jnp.concatenate([
-        latest((dst[None, :] == dst[:, None]) & early),
-        latest((slot[None, :] == slot[:, None]) & early),
-        latest(dst[None, :] == jnp.arange(own_count, dtype=jnp.int32)[:, None]),
-        latest(slot[None, :] == jnp.arange(size, dtype=jnp.int32)[:, None]),
-    ])
+    wanted = jnp.concatenate([
+        dst, slot, jnp.arange(own_count, dtype=jnp.int32), jnp.arange(size, dtype=jnp.int32)
+    ])[:, None]
+    by_dst = np.concatenate([np.ones(edges), np.zeros(edges), np.ones(own_count), np.zeros(size)]) > 0
+    free = np.full(own_count + size, edges)
+    before = np.concatenate([np.arange(edges), np.arange(edges), free])
+    e = np.arange(edges, dtype=np.int32)[None, :]
+    key = jnp.where(by_dst[:, None], dst[None, :], slot[None, :])
+    early = e < before[:, None]
+    found = jnp.max(jnp.where((key == wanted) & early, e, -1), axis=1)
+    return jnp.where(found < 0, edges, found)
 
 
 def grad_slot(split, own_count, t):
@@ -646,7 +648,7 @@
         run[e] = term(e) + run[prev(e)]
         return carry
 
-    lax.fori_loop(0, edges, one, 0, unroll=4)
+    lax.fori_loop(0, edges, one, 0, unroll=7)
 
 
 def spread(links, adj, dst, q, run):
@@ -657,8 +659,8 @@
     running(links.edges, run, lambda e: dot(adj[e], table[src[e]]), links.prev_dst)
 
 
-def send_out(links, own_count, run, gsend):
-    @pl.loop(0, gsend.shape[0])
+def send_out(links, own_count, run, gsend, first, last):
+    @pl.loop(first, last)
     def _(i):
         gsend[i] = run[links.last_slot(own_count + i)].astype(BF16)
 
@@ -692,7 +694,7 @@
         deg[b] = 1.0 + run_d[links.last_dst(b)]
         q[b] = (cot[b].astype(F32) / deg[b]).astype(BF16)
     spread(links, adj, dst, q, run_s)
-    send_out(links, own_count, run_s, first[0])
+    send_out(links, own_count, run_s, first[0], 0, place.nrow + place.nh * place.nx)
     await_all(place)
     send, pick = list_exchange(place, idx, tiles, picks, i_s, i_r)
     send()
@@ -701,7 +703,7 @@
         for b in range(own_count):
             u_own[b] = run_s[links.last_slot(b)] + q[b].astype(F32)
 
-    phase(place, CUT, feat, table1, u_back, picks, first, pick, lambda gsend: None, after_two, None)
+    phase(place, CUT, feat, table1, u_back, picks, first, pick, None, after_two, None)
 
     gather(links, adj, src, table1, run_d)
     for b in range(own_count):
@@ -722,7 +724,10 @@
 
     def fill_one(gsend):
         spread(links, adj, dst, q, run_s)
-        send_out(links, own_count, run_s, gsend)
+        send_out(links, own_count, run_s, gsend, place.nrow, place.nrow + place.nh * place.nx)
+
+    def fill_rows(gsend):
+        send_out(links, own_count, run_s, gsend, 0, place.nrow)
 
     def weights(b, total):
         dpre = keep[0, b]
@@ -740,7 +745,7 @@
         for b in range(own_count):
             base[b] = dot_bt(keep[0, b], ws1[...]) + q[b].astype(F32) + run_s[links.last_slot(b)]
 
-    phase(place, CUT, hidden, table2, back, picks, second, None, fill_one, after_one,
+    phase(place, CUT, hidden, table2, back, picks, second, None, (fill_one, fill_rows), after_one,
           sum_stages(place, grads, gout, rest))
 
 

time: 141 us -> 139 us (0.986)
  no operation moved by 1% of the time
where the time goes in v6:
time: 139 us; the launch traced here: 137 us
  Pallas kernels  132 us (95%)
  other arithmetic  3.52 us (3%)
    pallas_call x2, Pallas kernels, call(): pl.pallas_call(body, out_shape=out_shape, in_specs=[smem] * len(edges) +...  132 us

profile of v6, /device:TPU:1, one launch (start us, length us, event | category | flops | bytes accessed | tf_op | source)
XLA Modules:
  0.0 137.2 jit_solution(13557950031754528875)
XLA Ops:
  0.6 0.7 compare_select_fusion.1
  1.3 0.7 pad_add_fusion.1
  2.1 0.7 pad_add_fusion
  2.8 0.8 fusion
  3.6 0.6 compare_select_fusion.meta
  4.2 0.6 broadcast_in_dim.60.idx
  4.8 128.5 %shard_map.181 = (bf16[4,128,128]{2,1,0:T(8,128)(2,1)}, bf16[52,128,128]{2,1,0:T(8,128)(2,1)}, f32[4,128,128]{2,1,0:T(8,128)}, f32[4,128,128]{2,1,0:T(8,128)}, f...) custom-call(s32[28]{0:T(128)} %bitcast.16, s32[28]{0:T(128)} %bitcast.18, s32[112]{0:T(128)} %compare_select_fusion.meta, ...), custom_call_target="tpu_custom_call" | custom-call | tf_op jit(solution)/shard_map/pallas_call | solution.py:821
  133.3 4.0 %shard_map.182 = (bf16[4,128,128]{2,1,0:T(8,128)(2,1)}, f32[4,128,128]{2,1,0:T(8,128)}, f32[128,128]{1,0:T(8,128)}, f32[128,128]{1,0:T(8,128)}, f32[128,128]{1,0:T(8,128)}, /*index=5*/f32[128,128]{1,0:T(8,128)}) custom-call(s32[28]{0:T(128)} %bitcast.17, s32[28]{0:T(128)} %bitcast.19, s32[112]{0:T(128)} %compare_select_fusion.meta, ...), custom_call_target="tpu_custom_call" | custom-call | tf_op jit(solution)/shard_map/pallas_call | solution.py:821
  (3 shorter events, 0.0 us)
